TPU v7x, 128 devices: a whole 4x4x4 slice. The times are simulated.
128 devices in a mesh: cluster: 16 (over x, z), head: 8 (over y, core).
Axes of the slice: x: 4, y: 4, z: 4, core: 2. Of those that a mesh axis runs over, the one named last changes fastest.
Arguments:
- features: bfloat16 [16384, 1024], P(('cluster', 'head')), may hold values from -80 to 80
- grad_out: bfloat16 [16384, 1024], P(('cluster', 'head')), may hold values from -6 to 6
- w_qkv: bfloat16 [1024, 3072], replicated, may hold values from -0.1875 to 0.1875
- w_out: bfloat16 [1024, 1024], replicated, may hold values from -0.1875 to 0.1875
- kept_slot: int32 [128, 8], P('cluster'), may hold values from 0 to 55, as said below
- kept_count: int32 [128], P('cluster'), may hold values from 1 to 8, as said below
- fetch_slots: int32 [16, 16, 3], replicated, may hold values from 0 to 7, as said below
Outputs:
- attended: bfloat16 [16384, 1024], P(('cluster', 'head'))
- grad_features: bfloat16 [16384, 1024], P(('cluster', 'head'))
Inputs may be any that keep to these rules, and one draw needn't show every extreme that they name: fetch_slots[c, o] names 3 distinct blocks of cluster o, numbered 0 to 7 within o, that cluster c reads; every pair has exactly 3; the row o = c is never read. `kept_slot`: a position in the table of query block b's cluster c: below 8 the block of c of that number, else position 8 + o * 3 + r stands for fetch_slots[c, o, r], with o never c; entry 0 is the query block's own block; the entries of a row are distinct. `kept_count`: some query block keeps all 8 entries; clusters differ in how many they keep.
All inputs are finite; a program needn't handle non-finite values.
Results may differ from a plain program's by a relative error of at most 0.024.
The roundings to bfloat16 on the way count: a program that leaves them out, or rounds other values in their place, can miss the bound.
Values may be sent and summed in bfloat16 or wider, within the bound.
A program may use at most 128 MiB of HBM per device.

v0:
```python
import math

import jax
import jax.numpy as jnp
from jax import lax
from jax.sharding import PartitionSpec as P

HEADS = 16
HD = 64
BLK = 128


def shards(features, grad_out, w_qkv, w_out, kept_slot, kept_count, fetch_slots):
    rows_dev, model_width = features.shape
    head_count = lax.axis_size("head")
    cluster_count = lax.axis_size("cluster")
    cluster = lax.axis_index("cluster")
    own_blocks, kept_width = kept_slot.shape
    slot_count = fetch_slots.shape[2]
    local_heads = HEADS // head_count
    head_cols = local_heads * HD
    cluster_rows = rows_dev * head_count
    score_scale = 1.0 / math.sqrt(HD)
    group_size = 4
    group_count = own_blocks // group_size
    qkv_rows = jnp.dot(features, w_qkv, preferred_element_type=jnp.float32).astype(jnp.bfloat16)
    grad_attn = lax.dot_general(
        grad_out, w_out, (((1,), (1,)), ((), ())), preferred_element_type=jnp.float32
    ).astype(jnp.bfloat16)
    packed = jnp.concatenate([qkv_rows, grad_attn], axis=1).reshape(
        rows_dev, 4, head_count, head_cols
    )
    regrouped = lax.all_to_all(packed, "head", split_axis=2, concat_axis=0, tiled=True)
    regrouped = regrouped.reshape(own_blocks, BLK, 4, local_heads, HD)
    queries = regrouped[:, :, 0]
    grad_heads = regrouped[:, :, 3]
    key_value = regrouped[:, :, 1:3]
    kv_table = lax.all_gather(key_value, "cluster", axis=0, tiled=True)
    own_lists = lax.dynamic_index_in_dim(fetch_slots, cluster, 0, keepdims=False)
    fetched = jnp.maximum(kept_slot - own_blocks, 0)
    source = fetched // slot_count
    within = fetched % slot_count
    remote = own_lists[source, within]
    pick_ids = jnp.where(
        kept_slot < own_blocks, cluster * own_blocks + kept_slot, source * own_blocks + remote
    )
    live_mask = jnp.arange(kept_width, dtype=jnp.int32)[None, :] < kept_count[:, None]

    def group_work(items):
        query_group, grad_group, id_group, live_group = items
        picked = kv_table[id_group]
        key_pick = picked[:, :, :, 0]
        value_pick = picked[:, :, :, 1]
        scores = (
            jnp.einsum(
                "bqhd,bjkhd->bhqjk", query_group, key_pick, preferred_element_type=jnp.float32
            )
            * score_scale
        )
        scores = jnp.where(live_group[:, None, None, :, None], scores, -jnp.inf)
        top_score = jnp.max(scores, axis=(3, 4), keepdims=True)
        raised = jnp.exp(scores - top_score)
        attention = raised / jnp.sum(raised, axis=(3, 4), keepdims=True)
        attention_low = attention.astype(jnp.bfloat16)
        attn_group = jnp.einsum(
            "bhqjk,bjkhd->bqhd", attention_low, value_pick, preferred_element_type=jnp.float32
        ).astype(jnp.bfloat16)
        grad_probs = jnp.einsum(
            "bqhd,bjkhd->bhqjk", grad_group, value_pick, preferred_element_type=jnp.float32
        )
        row_delta = jnp.moveaxis(
            jnp.sum(grad_group.astype(jnp.float32) * attn_group.astype(jnp.float32), axis=-1), 2, 1
        )
        grad_scores = (attention * (grad_probs - row_delta[..., None, None]) * score_scale).astype(
            jnp.bfloat16
        )
        grad_query = jnp.einsum(
            "bhqjk,bjkhd->bqhd", grad_scores, key_pick, preferred_element_type=jnp.float32
        ).astype(jnp.bfloat16)
        key_terms = jnp.einsum(
            "bhqjk,bqhd->bjkhd", grad_scores, query_group, preferred_element_type=jnp.float32
        )
        value_terms = jnp.einsum(
            "bhqjk,bqhd->bjkhd", attention_low, grad_group, preferred_element_type=jnp.float32
        )
        return (attn_group, grad_query, jnp.stack([key_terms, value_terms], axis=3))

    def grouped(array):
        return array.reshape((group_count, group_size) + array.shape[1:])

    attn_out, grad_query, block_grads = lax.map(
        group_work, (grouped(queries), grouped(grad_heads), grouped(pick_ids), grouped(live_mask))
    )
    attn_out = attn_out.reshape(own_blocks, BLK, local_heads, HD)
    grad_query = grad_query.reshape(own_blocks, BLK, local_heads, HD)
    feature_size = BLK * 2 * head_cols
    block_grads = block_grads.reshape(own_blocks * kept_width, feature_size)
    flat_ids = pick_ids.reshape(-1)
    everything = (
        jnp.zeros((own_blocks * cluster_count, feature_size), jnp.float32)
        .at[flat_ids]
        .add(block_grads)
    )
    kv_grads = lax.psum_scatter(
        everything.astype(jnp.bfloat16), "cluster", scatter_dimension=0, tiled=True
    )
    kv_low = kv_grads.reshape(own_blocks, BLK, 2, local_heads, HD)
    back_rows = jnp.concatenate([attn_out[:, :, None], grad_query[:, :, None], kv_low], axis=2)
    back_rows = back_rows.reshape(cluster_rows, 4, 1, head_cols)
    restored = lax.all_to_all(back_rows, "head", split_axis=0, concat_axis=2, tiled=True).reshape(
        rows_dev, 4 * model_width
    )
    attended = jnp.dot(restored[:, :model_width], w_out, preferred_element_type=jnp.float32).astype(
        jnp.bfloat16
    )
    grad_features = lax.dot_general(
        restored[:, model_width:],
        w_qkv,
        (((1,), (1,)), ((), ())),
        preferred_element_type=jnp.float32,
    ).astype(jnp.bfloat16)
    return (attended, grad_features)


def solution(mesh):
    in_specs = (
        P(("cluster", "head"), None),
        P(("cluster", "head"), None),
        P(),
        P(),
        P("cluster", None),
        P("cluster"),
        P(),
    )
    out_specs = (P(("cluster", "head"), None), P(("cluster", "head"), None))
    return jax.shard_map(shards, mesh=mesh, in_specs=in_specs, out_specs=out_specs, check_vma=False)
```

profile of v0, /device:TPU:1, one launch (start us, length us, event | category | flops | bytes accessed | tf_op | source)
XLA Modules:
  0.0 406.1 jit_solution(5873491580082928292)
XLA Ops:
  8.8 1.8 convolution_convert_fusion.3
  10.5 3.9 convolution_convert_fusion
  14.8 1.7 copy.69
  16.5 21.2 %all_to_all.30 = bf16[128,4,8,128]{0,3,1,2:T(8,128)(2,1)S(1)} all-to-all(bf16[128,4,8,128]{0,3,1,2:T(8,128)(2,1)} %copy.69), channel_id=1, replica_groups=mesh['cluster'=16,'head'=8] {'head'}, dimensions={2} | all-to-all | bytes 2097152 | tf_op jit(solution)/shard_map/all_to_all | solution.py:33
  42.2 68.1 %all-gather.2.cloned.1.call-done = bf16[128,128,2,2,64]{1,4,3,2,0:T(8,128)(2,1)} async-done(((bf16[8,128,2,2,64]{1,4,3,2,0:T(8,128)(2,1)}), bf16[128,128,2,2,64]{1,4,3,2,0:T(8,128)(2,1)}) %all-gather.2.cloned.1.call-update) | async-done | bytes 8388624 | tf_op jit(solution)/shard_map/all_gather | solution.py:38
  110.3 41.3 %while.14 = (s32[]{:T(128)}, bf16[2,4,128,2,64]{2,4,3,1,0:T(8,128)(2,1)}, bf16[2,4,128,2,64]{2,4,3,1,0:T(8,128)(2,1)}, f32[2,4,8,128,2,2,64]{3,6,2,5,1,4,0:T(8,1...) while((s32[]{:T(128)}, ...), condition=%wide.region_4.5_spmd, body=%wide.region_0.4_spmd.sunk | while | flops 832960640 | bytes 117624000 | solution.py:91
  110.4 5.6 %gather_fusion = bf16[32,128,2,2,64]{1,4,3,2,0:T(8,128)(2,1)} fusion(bf16[128,128,2,2,64]{1,4,3,2,0:T(8,128)(2,1)} %get-tuple-element.181, s32[1024]{0:T(1024)S(1)} %pad_clamp_fusion.2), kind=kCustom, calls=%fused_computation.clone.1 | custom fusion | bytes 4194432 | tf_op jit(solution)/shard_map/while/body/eval_jaxpr/gather | solution.py:51
  116.0 1.7 fusion.63
  121.3 2.2 multiply_convert_fusion.2
  127.8 3.2 copy-done.1
  131.1 5.6 %gather_fusion = bf16[32,128,2,2,64]{1,4,3,2,0:T(8,128)(2,1)} fusion(bf16[128,128,2,2,64]{1,4,3,2,0:T(8,128)(2,1)} %get-tuple-element.181, s32[1024]{0:T(1024)S(1)} %pad_clamp_fusion.2), kind=kCustom, calls=%fused_computation.clone.1 | custom fusion | bytes 4194432 | tf_op jit(solution)/shard_map/while/body/eval_jaxpr/gather | solution.py:51
  142.0 2.2 multiply_convert_fusion.2
  148.4 3.2 copy-done.1
  151.6 23.1 %copy.72 = f32[2,4,8,128,2,2,64]{6,5,4,3,2,1,0:T(2,128)} copy(f32[2,4,8,128,2,2,64]{3,6,2,5,1,4,0:T(8,128)} %get-tuple-element.53) | data formatting | bytes 16777216 | tf_op jit(solution)/shard_map/while | solution.py:91
  174.7 18.4 %reshape.127 = f32[64,32768]{1,0:T(8,128)} reshape(f32[2,4,8,128,2,2,64]{6,5,4,3,2,1,0:T(2,128)} %copy.72) | data formatting | bytes 16777216 | tf_op jit(solution)/shard_map/reshape | solution.py:97
  193.2 19.3 %scatter_custom_fusion = f32[128,32768]{1,0:T(8,128)} fusion(s32[64]{0:T(128)} %fusion.35, f32[64,32768]{1,0:T(8,128)} %reshape.127, f32[]{:T(128)} %constant.42.clone.1), kind=kCustom, calls=%fused_computation.41 | custom fusion | flops 2097152 | bytes 16777728 | tf_op jit(solution)/shard_map/scatter-add | solution.py:102
  212.5 8.9 %convert_element_type.41 = bf16[128,32768]{1,0:T(8,128)(2,1)} convert(f32[128,32768]{1,0:T(8,128)} %scatter_custom_fusion) | non-fusion elementwise | flops 4194304 | bytes 25165824 | tf_op jit(solution)/shard_map/convert_element_type | solution.py:105
  225.3 2.5 reshape.148
  227.8 134.6 %all-reduce.3.cloned.1.call-done = bf16[128,32768]{1,0:T(8,128)(2,1)} async-done(((bf16[128,32768]{1,0:T(8,128)(2,1)}), bf16[128,32768]{1,0:T(8,128)(2,1)}) %all-reduce.3.cloned.1.call-update) | async-done | bytes 8388624
  362.5 1.9 constant_dynamic-slice_fusion
  364.4 2.2 concatenate.20
  366.6 2.8 maximum_bitcast_fusion.2
  369.4 20.3 %all_to_all.31 = bf16[1024,4,1,128]{3,1,2,0:T(4,128)(2,1)S(1)} all-to-all(bf16[1024,4,1,128]{3,1,2,0:T(4,128)(2,1)S(1)} %maximum_bitcast_fusion.2), channel_id=1, replica_groups=mesh['cluster'=16,'head'=8] {'head'}, dimensions={0} | all-to-all | bytes 2097152 | tf_op jit(solution)/shard_map/all_to_all | solution.py:110
  393.6 5.7 %convolution_convert_fusion.1 = bf16[128,1024]{1,0:T(8,128)(2,1)} fusion(bf16[1024,3072]{1,0:T(8,128)(2,1)} %param.11, bf16[128,4096]{0,1:T(8,128)(2,1)S(1)} %bitcast.159), kind=kOutput, calls=%fused_computation.44 | convolution fusion | flops 805437440 | bytes 7340032 | tf_op jit(solution)/shard_map/dot_general | solution.py:116
  (98 shorter events, 30.8 us)
Async XLA Ops:
  7.2 1.6 copy-start
  7.2 103.1 %all-gather.2.cloned.1.call-start = ((), (), s32[]{:S(2)}) async-start(), calls=%async_computation.2 | async-start | bytes 8912896 | tf_op jit(solution)/shard_map/all_gather | solution.py:38
  14.5 25.1 %copy-start.9 = (s32[8,8]{1,0:T(8,128)S(1)}, s32[8,8]{1,0:T(8,128)}, u32[]{:S(2)}) copy-start(s32[8,8]{1,0:T(8,128)} %param.13) | copy-start | bytes 772
  16.5 24.2 %copy-start.10 = (s32[8]{0:T(128)S(1)}, s32[8]{0:T(128)}, u32[]{:S(2)}) copy-start(s32[8]{0:T(128)} %param.14) | copy-start | bytes 100
  38.6 323.9 %all-reduce.3.cloned.1.call-start = ((), (), s32[]{:S(2)}) async-start(), calls=%async_computation.3 | async-start | bytes 16777216
  117.7 2.1 copy-start.3
  119.8 1.4 copy-start.2
  121.2 2.3 copy-start.4
  121.3 2.2 copy-start.6
  123.5 3.0 slice-start
  124.1 1.5 copy-start.7
  124.1 3.1 slice-start.1
  127.8 3.2 copy-start.1
  138.4 2.1 copy-start.3
  140.5 1.4 copy-start.2
  141.9 2.3 copy-start.4
  142.0 2.2 copy-start.6
  144.2 3.0 slice-start
  144.7 1.5 copy-start.7
  144.8 3.1 slice-start.1
  148.4 3.2 copy-start.1
  221.3 0.7 copy-start.11
  221.3 2.0 copy-start.8
  221.3 2.8 copy-start.5
Sparse Core Ops, SparseCore 0:
  38.7 71.5 all-gather.1
  221.5 140.9 all-reduce.2
where the time goes:
time: 408 us; the launch traced here: 406 us
  waiting for transfers between devices  203 us (50%)
  local copies, waits for them, and re-layouts  83.9 us (21%)
  blocking collectives  41.5 us (10%)
  other arithmetic  34.8 us (9%)
  matrix products  27.7 us (7%)
  between operations  14.9 us (4%)
    unnamed x3, waiting for transfers between devices  135 us
    all_gather x1, waiting for transfers between devices, shards(): kv_table = lax.all_gather(key_value, 'cluster', axis=0, tiled=True)  68.1 us
    while x1, local copies, waits for them, and re-layouts, shards(): lax.map(group_work, (grouped(queries), grouped(grad_heads), grouped(pick_...  23.1 us
    all_to_all x1, blocking collectives, shards(): lax.all_to_all(packed, 'head', split_axis=2, concat_axis=0, tiled=True)  21.2 us
    all_to_all x1, blocking collectives, shards(): lax.all_to_all(back_rows, 'head', split_axis=0, concat_axis=2, tiled=True)  20.3 us
    scatter-add x1, other arithmetic, shards(): everything = jnp.zeros((own_blocks * cluster_count, feature_size), jnp.fl...  19.3 us
    reshape x1, local copies, waits for them, and re-layouts, shards(): block_grads = block_grads.reshape(own_blocks * kept_width, feature_size)  18.4 us
    gather x2, local copies, waits for them, and re-layouts, group_work(): picked = kv_table[id_group]  11.1 us
  transfers between devices with their start and end apart: 2, of which 2 were waited for; matrix products, arithmetic and copies ran while one was open for 2% of the time, Pallas kernels for 0%

commit v1 on v0

v1 whole, which is shorter than its diff:
```python
import functools

import jax
import jax.numpy as jnp
from jax import lax
from jax.experimental import pallas as pl
from jax.experimental.pallas import tpu as pltpu
from jax.sharding import PartitionSpec as P

MESH = pl.DeviceIdType.MESH
BF = jnp.bfloat16
F32 = jnp.float32
BLK = 128
NB = 8
SIDE = 4
SLOT = 3
FAR = (1, 3, 2)
VMEM_LIMIT = 56 << 20

NN = (((1,), (0,)), ((), ()))
NT = (((1,), (1,)), ((), ()))


def dot(a, b, dims=NN):
    return lax.dot_general(a, b, dims, preferred_element_type=F32)


def place():
    c = lax.axis_index("cluster")
    h = lax.axis_index("head")
    return c // SIDE, c % SIDE, h


def greet(x, z, h):
    barrier = pltpu.get_barrier_semaphore()
    for d in (1, 2, 3):
        pl.semaphore_signal(
            barrier, inc=1, device_id=(lax.rem(x + d, SIDE) * SIDE + z, h), device_id_type=MESH
        )
        pl.semaphore_signal(
            barrier, inc=1, device_id=(x * SIDE + lax.rem(z + d, SIDE), h), device_id_type=MESH
        )
    for d in range(1, NB):
        pl.semaphore_signal(
            barrier, inc=1, device_id=(x * SIDE + z, lax.rem(h + d, NB)), device_id_type=MESH
        )
    pl.semaphore_wait(barrier, 6 + NB - 1)


def forward_kernel(
    feat, gout, wqkv, wout, fetch,
    q_all, g_all, gk0, gk1, gk2, gk3, tk1, tk2, tk3, gv0, gv1, gv2, gv3, tv1, tv2, tv3,
    wk_v, wv_v, wq_v, wo_v, sendbuf, stage_k, stage_v,
    w_sem, y_send, y_recv, k_send, k_recv, v_send, v_recv, k2_send, k2_recv, v2_send, v2_recv,
):
    x, z, h = place()
    cluster = x * SIDE + z
    gk = (gk0, gk1, gk2, gk3)
    gv = (gv0, gv1, gv2, gv3)
    tk = (None, tk1, tk2, tk3)
    tv = (None, tv1, tv2, tv3)
    loads = [
        pltpu.make_async_copy(wqkv.at[:, pl.ds(1024, 1024)], wk_v, w_sem.at[0]),
        pltpu.make_async_copy(wqkv.at[:, pl.ds(2048, 1024)], wv_v, w_sem.at[1]),
        pltpu.make_async_copy(wqkv.at[:, pl.ds(0, 1024)], wq_v, w_sem.at[2]),
        pltpu.make_async_copy(wout, wo_v, w_sem.at[3]),
    ]
    for load in loads:
        load.start()
    greet(x, z, h)

    def project(part, rows, weight, dims, own):
        for p in range(4):
            if dims is NN:
                w = weight[:, p * 256 : (p + 1) * 256]
            else:
                w = weight[p * 256 : (p + 1) * 256, :]
            out = dot(rows[...], w, dims).astype(BF)
            sendbuf[part, 2 * p] = out[:, :128]
            sendbuf[part, 2 * p + 1] = out[:, 128:]
        own[h] = sendbuf[part, h]

    def y_copies(part, own):
        copies = []
        for d in range(1, NB):
            to = lax.rem(h + d, NB)
            copies.append(
                pltpu.make_async_remote_copy(
                    sendbuf.at[part, to], own.at[h], y_send.at[part, d - 1], y_recv.at[part, d - 1],
                    device_id=(cluster, to), device_id_type=MESH,
                )
            )
        return copies

    def recv_y(part, own):
        for d in range(1, NB):
            frm = lax.rem(h - d + NB, NB)
            pltpu.make_async_remote_copy(
                sendbuf.at[part, frm], own.at[frm], y_send.at[part, d - 1], y_recv.at[part, d - 1],
                device_id=(cluster, frm), device_id_type=MESH,
            ).wait_recv()

    loads[0].wait()
    project(0, feat, wk_v, NN, gk0)
    ycopy_k = y_copies(0, gk0)
    for copy in ycopy_k:
        copy.start()
    loads[1].wait()
    project(1, feat, wv_v, NN, gv0)
    ycopy_v = y_copies(1, gv0)
    for copy in ycopy_v:
        copy.start()
    loads[2].wait()
    project(2, feat, wq_v, NN, q_all)
    loads[3].wait()
    project(3, gout, wo_v, NT, g_all)

    def x_dev(d):
        return (lax.rem(x - d + SIDE, SIDE) * SIDE + z, h)

    def z_dev(d):
        return (x * SIDE + lax.rem(z - d + SIDE, SIDE), h)

    def first(own, dests, dev, send, recv):
        copies = {}
        for d in FAR:
            copies[d] = pltpu.make_async_remote_copy(
                own, dests[d], send.at[d - 1], recv.at[d - 1], device_id=dev(d), device_id_type=MESH
            )
            copies[d].start()
        return copies

    def second_k(e):
        copies = []
        source = lax.rem(x + e, SIDE) * SIDE + z
        for d in FAR:
            reader = x * SIDE + lax.rem(z - d + SIDE, SIDE)
            for r in range(SLOT):
                stage_k[d - 1, e, r] = gk[e][fetch[reader, source, r]]
            copy = pltpu.make_async_remote_copy(
                stage_k.at[d - 1, e], tk[d].at[e], k2_send.at[d - 1, e], k2_recv.at[d - 1, e],
                device_id=z_dev(d), device_id_type=MESH,
            )
            copy.start()
            copies.append(copy)
        return copies

    def second_v(e):
        copies = []
        source = x * SIDE + lax.rem(z + e, SIDE)
        for d in FAR:
            reader = lax.rem(x - d + SIDE, SIDE) * SIDE + z
            for r in range(SLOT):
                stage_v[d - 1, e, r] = gv[e][fetch[reader, source, r]]
            copy = pltpu.make_async_remote_copy(
                stage_v.at[d - 1, e], tv[d].at[e], v2_send.at[d - 1, e], v2_recv.at[d - 1, e],
                device_id=x_dev(d), device_id_type=MESH,
            )
            copy.start()
            copies.append(copy)
        return copies

    recv_y(0, gk0)
    copies_k = first(gk0, gk, x_dev, k_send, k_recv)
    seconds = second_k(0)
    recv_y(1, gv0)
    copies_v = first(gv0, gv, z_dev, v_send, v_recv)
    seconds += second_v(0)
    ycopy_q = y_copies(2, q_all)
    ycopy_g = y_copies(3, g_all)
    for copy in ycopy_q + ycopy_g:
        copy.start()
    for e in FAR:
        copies_k[e].wait_recv()
        seconds += second_k(e)
        copies_v[e].wait_recv()
        seconds += second_v(e)
    recv_y(2, q_all)
    recv_y(3, g_all)
    for copy in ycopy_k + ycopy_v + ycopy_q + ycopy_g:
        copy.wait_send()
    for d in FAR:
        copies_k[d].wait_send()
        copies_v[d].wait_send()
    for copy in seconds:
        copy.wait()


def attention_kernel(
    kept, count, fetch, q_all, g_all,
    gk0, gk1, gk2, gk3, tk1, tk2, tk3, gv0, gv1, gv2, gv3, tv1, tv2, tv3,
    attn_out, dq_out, dkg, dkt, dvg, dvt,
    kt, vt, dk, dv, sem,
):
    x, z, h = place()
    cluster = x * SIDE + z
    copies = []
    for n, (table, parts) in enumerate(
        ((kt, (gk0, gk1, gk2, gk3, tk1, tk2, tk3)), (vt, (gv0, gv1, gv2, gv3, tv1, tv2, tv3)))
    ):
        at = 0
        for m, part in enumerate(parts):
            rows = part.shape[0]
            copies.append(
                pltpu.make_async_copy(part, table.at[pl.ds(at, rows)], sem.at[n, m])
            )
            at += rows
    for copy in copies:
        copy.start()

    def clear(i, _):
        dk[i] = jnp.zeros((BLK, BLK), F32)
        dv[i] = jnp.zeros((BLK, BLK), F32)
        return 0

    lax.fori_loop(0, 68, clear, 0)
    for copy in copies:
        copy.wait()
    lane = lax.broadcasted_iota(jnp.int32, (BLK, BLK), 1)
    low = lane < 64

    def block(b, _):
        n = count[b]
        k_at, v_at = [], []
        for j in range(NB):
            t = jnp.where(j < n, kept[b, j], b)
            s = jnp.maximum(t - NB, 0)
            o = s // SLOT
            r = s - o * SLOT
            e = lax.rem(o // SIDE - x + SIDE, SIDE)
            f = lax.rem(o % SIDE - z + SIDE, SIDE)
            blk = fetch[cluster, o, r]
            k_far = jnp.where(f == 0, e * NB + blk, 32 + (f - 1) * 12 + e * SLOT + r)
            v_far = jnp.where(e == 0, f * NB + blk, 32 + (e - 1) * 12 + f * SLOT + r)
            k_at.append(jnp.where(t < NB, t, k_far))
            v_at.append(jnp.where(t < NB, t, v_far))
        kc = jnp.concatenate([kt[i] for i in k_at], axis=0)
        vc = jnp.concatenate([vt[i] for i in v_at], axis=0)
        q = q_all[b].astype(F32) * 0.125
        g = g_all[b].astype(F32)
        q_t = q.T.astype(BF)
        g_t = g.T.astype(BF)
        zero = jnp.zeros_like(q)
        probs, lows, outs = [], [], []
        for hh in range(2):
            mine = low if hh == 0 else jnp.logical_not(low)
            qh = jnp.where(mine, q, zero).astype(BF)
            s = dot(qh, kc, NT)
            s = jnp.concatenate(
                [jnp.where(j < n, s[:, j * BLK : (j + 1) * BLK], -jnp.inf) for j in range(NB)],
                axis=1,
            )
            p = jnp.exp(s - jnp.max(s, axis=1, keepdims=True))
            a = p * (1.0 / jnp.sum(p, axis=1, keepdims=True))
            al = a.astype(BF)
            probs.append(a)
            lows.append(al)
            outs.append(dot(al, vc))
        attn = jnp.where(low, outs[0], outs[1]).astype(BF)
        attn_out[b] = attn
        prod = g * attn.astype(F32)
        dqs = []
        for hh in range(2):
            mine = low if hh == 0 else jnp.logical_not(low)
            delta = jnp.sum(jnp.where(mine, prod, zero), axis=1, keepdims=True)
            gh = jnp.where(mine, g, zero).astype(BF)
            ds = (probs[hh] * (dot(gh, vc, NT) - delta)).astype(BF)
            dqs.append(dot(ds, kc))
            half = slice(hh * 64, (hh + 1) * 64)
            dk_t = dot(q_t[half], ds)
            dv_t = dot(g_t[half], lows[hh])
            for j in range(NB):
                cols = slice(j * BLK, (j + 1) * BLK)
                dk[k_at[j], half, :] += dk_t[:, cols]
                dv[v_at[j], half, :] += dv_t[:, cols]
        dq_out[b] = (jnp.where(low, dqs[0], dqs[1]) * 0.125).astype(BF)
        return 0

    lax.fori_loop(0, NB, block, 0)

    def flush_g(i, _):
        dkg[i] = dk[i]
        dvg[i] = dv[i]
        return 0

    def flush_t(i, _):
        dkt[i] = dk[i + 32].astype(BF)
        dvt[i] = dv[i + 32].astype(BF)
        return 0

    lax.fori_loop(0, 32, flush_g, 0)
    lax.fori_loop(0, 36, flush_t, 0)


def backward_kernel(
    fetch, attn, dq, dkg, dkt, dvg, dvt, wqkv, wout,
    attended, grad_features,
    rk0, rk1, rk2, rk3, rv0, rv1, rv2, rv3, sum_k, sum_v, back_k, back_v, own_k, own_v,
    attn_all, dq_all, dk_all, dv_all, wk_v, wv_v, wq_v, wo_v,
    w_sem, y_send, y_recv, k_send, k_recv, v_send, v_recv, k2_send, k2_recv, v2_send, v2_recv,
):
    x, z, h = place()
    cluster = x * SIDE + z
    rk = (rk0, rk1, rk2, rk3)
    rv = (rv0, rv1, rv2, rv3)
    loads = [
        pltpu.make_async_copy(wout, wo_v, w_sem.at[3]),
        pltpu.make_async_copy(wqkv.at[:, pl.ds(0, 1024)], wq_v, w_sem.at[2]),
        pltpu.make_async_copy(wqkv.at[:, pl.ds(1024, 1024)], wk_v, w_sem.at[0]),
        pltpu.make_async_copy(wqkv.at[:, pl.ds(2048, 1024)], wv_v, w_sem.at[1]),
    ]
    for load in loads:
        load.start()
    for ref in rk + rv:
        ref[12] = jnp.zeros((BLK, BLK), BF)
    greet(x, z, h)

    def x_dev(d):
        return (lax.rem(x + d, SIDE) * SIDE + z, h)

    def z_dev(d):
        return (x * SIDE + lax.rem(z + d, SIDE), h)

    def chunk(src, dests, dev, e, d, send, recv):
        return pltpu.make_async_remote_copy(
            src.at[pl.ds(((d - 1) * SIDE + e) * SLOT, SLOT)],
            dests[e].at[pl.ds((d - 1) * SLOT, SLOT)],
            send.at[d - 1, e], recv.at[d - 1, e],
            device_id=dev(d), device_id_type=MESH,
        )

    order = (2, 1, 3, 0)
    firsts = {}
    for e in order:
        for d in FAR:
            ck = chunk(dkt, rk, z_dev, e, d, k_send, k_recv)
            cv = chunk(dvt, rv, x_dev, e, d, v_send, v_recv)
            ck.start()
            cv.start()
            firsts[e, d] = (ck, cv)

    def y_copies(part, src, dest):
        copies = []
        for d in range(1, NB):
            to = lax.rem(h + d, NB)
            copies.append(
                pltpu.make_async_remote_copy(
                    src.at[to], dest.at[h], y_send.at[part, d - 1], y_recv.at[part, d - 1],
                    device_id=(cluster, to), device_id_type=MESH,
                )
            )
        for copy in copies:
            copy.start()
        dest[h] = src[h]
        return copies

    def recv_y(part, src, dest):
        for d in range(1, NB):
            frm = lax.rem(h - d + NB, NB)
            pltpu.make_async_remote_copy(
                src.at[frm], dest.at[frm], y_send.at[part, d - 1], y_recv.at[part, d - 1],
                device_id=(cluster, frm), device_id_type=MESH,
            ).wait_recv()

    ycopies = y_copies(0, attn, attn_all) + y_copies(1, dq, dq_all)

    def gathered(ref):
        return jnp.concatenate([ref[i] for i in range(NB)], axis=1)

    recv_y(0, attn, attn_all)
    loads[0].wait()
    attended[...] = dot(gathered(attn_all), wo_v[...]).astype(BF)
    recv_y(1, dq, dq_all)
    loads[1].wait()
    grad = dot(gathered(dq_all), wq_v[...], NT)

    def where_is(reader, source, blk, d):
        at = jnp.int32(12)
        for r in range(SLOT):
            at = jnp.where(fetch[reader, source, r] == blk, (d - 1) * SLOT + r, at)
        return at

    def total(e, base, got, reader_of, source, out):
        def one(blk, _):
            acc = base[e * NB + blk]
            for d in (1, 2, 3):
                acc = acc + got[e][where_is(reader_of(d), source, blk, d)].astype(F32)
            out(blk, acc)
            return 0

        lax.fori_loop(0, NB, one, 0)

    backs = []
    for e in order:
        for d in FAR:
            firsts[e, d][0].wait_recv()

        def put_k(blk, acc, e=e):
            if e == 0:
                own_k[blk] = acc
            else:
                sum_k[e - 1, blk] = acc.astype(BF)

        total(
            e, dkg, rk, lambda d: x * SIDE + lax.rem(z - d + SIDE, SIDE),
            lax.rem(x + e, SIDE) * SIDE + z, put_k,
        )
        if e:
            copy = pltpu.make_async_remote_copy(
                sum_k.at[e - 1], back_k.at[e - 1], k2_send.at[e - 1], k2_recv.at[e - 1],
                device_id=x_dev(e), device_id_type=MESH,
            )
            copy.start()
            backs.append(copy)
        for d in FAR:
            firsts[e, d][1].wait_recv()

        def put_v(blk, acc, e=e):
            if e == 0:
                own_v[blk] = acc
            else:
                sum_v[e - 1, blk] = acc.astype(BF)

        total(
            e, dvg, rv, lambda d: lax.rem(x - d + SIDE, SIDE) * SIDE + z,
            x * SIDE + lax.rem(z + e, SIDE), put_v,
        )
        if e:
            copy = pltpu.make_async_remote_copy(
                sum_v.at[e - 1], back_v.at[e - 1], v2_send.at[e - 1], v2_recv.at[e - 1],
                device_id=z_dev(e), device_id_type=MESH,
            )
            copy.start()
            backs.append(copy)

    for copy in backs:
        copy.wait()

    def finish(own, back, out):
        def one(blk, _):
            acc = own[blk]
            for d in range(3):
                acc = acc + back[d, blk].astype(F32)
            out[blk] = acc.T.astype(BF)
            return 0

        lax.fori_loop(0, NB, one, 0)

    finish(own_k, back_k, sum_k.at[0])
    ycopies += y_copies(2, sum_k.at[0], dk_all)
    finish(own_v, back_v, sum_v.at[0])
    ycopies += y_copies(3, sum_v.at[0], dv_all)
    recv_y(2, sum_k.at[0], dk_all)
    loads[2].wait()
    grad = grad + dot(gathered(dk_all), wk_v[...], NT)
    recv_y(3, sum_v.at[0], dv_all)
    loads[3].wait()
    grad = grad + dot(gathered(dv_all), wv_v[...], NT)
    grad_features[...] = grad.astype(BF)
    for copy in ycopies:
        copy.wait_send()
    for pair in firsts.values():
        pair[0].wait_send()
        pair[1].wait_send()


def vmem():
    return pl.BlockSpec(memory_space=pltpu.VMEM)


def anym():
    return pl.BlockSpec(memory_space=pl.ANY)


def smem():
    return pl.BlockSpec(memory_space=pltpu.SMEM)


def shards(features, grad_out, w_qkv, w_out, kept_slot, kept_count, fetch_slots):
    dma = pltpu.SemaphoreType.DMA
    tile = (BLK, BLK)
    own = jax.ShapeDtypeStruct((NB,) + tile, BF)
    far = jax.ShapeDtypeStruct((SIDE, SLOT) + tile, BF)
    weights = [pltpu.VMEM((1024, 1024), BF) for _ in range(4)]
    moved = pl.pallas_call(
        forward_kernel,
        out_shape=[own, own] + ([own] * 4 + [far] * 3) * 2,
        in_specs=[vmem(), vmem(), anym(), anym(), smem()],
        out_specs=[vmem()] * 16,
        scratch_shapes=weights
        + [
            pltpu.VMEM((4, NB) + tile, BF),
            pltpu.VMEM((3, SIDE, SLOT) + tile, BF),
            pltpu.VMEM((3, SIDE, SLOT) + tile, BF),
            dma((4,)), dma((4, NB - 1)), dma((4, NB - 1)),
            dma((3,)), dma((3,)), dma((3,)), dma((3,)),
            dma((3, SIDE)), dma((3, SIDE)), dma((3, SIDE)), dma((3, SIDE)),
        ],
        compiler_params=pltpu.CompilerParams(
            collective_id=0, has_side_effects=True, vmem_limit_bytes=VMEM_LIMIT
        ),
    )(features, grad_out, w_qkv, w_out, fetch_slots)
    q_all, g_all = moved[:2]
    tables = [m.reshape((-1,) + tile) for m in moved[2:]]
    wide = jax.ShapeDtypeStruct((32,) + tile, F32)
    slim = jax.ShapeDtypeStruct((36,) + tile, BF)
    attn, dq, dkg, dkt, dvg, dvt = pl.pallas_call(
        attention_kernel,
        out_shape=[own, own, wide, slim, wide, slim],
        in_specs=[smem()] * 3 + [vmem()] * 2 + [anym()] * 14,
        out_specs=[vmem()] * 6,
        scratch_shapes=[
            pltpu.VMEM((68,) + tile, BF),
            pltpu.VMEM((68,) + tile, BF),
            pltpu.VMEM((68,) + tile, F32),
            pltpu.VMEM((68,) + tile, F32),
            dma((2, 7)),
        ],
        compiler_params=pltpu.CompilerParams(vmem_limit_bytes=VMEM_LIMIT),
    )(kept_slot, kept_count, fetch_slots, q_all, g_all, *tables)
    rows, width = features.shape
    got = [pltpu.VMEM((13,) + tile, BF) for _ in range(8)]
    return pl.pallas_call(
        backward_kernel,
        out_shape=[jax.ShapeDtypeStruct((rows, width), BF)] * 2,
        in_specs=[smem()] + [vmem()] * 6 + [anym()] * 2,
        out_specs=[vmem()] * 2,
        scratch_shapes=got
        + [pltpu.VMEM((3, NB) + tile, BF) for _ in range(4)]
        + [pltpu.VMEM((NB,) + tile, F32) for _ in range(2)]
        + [pltpu.VMEM((NB,) + tile, BF) for _ in range(4)]
        + weights
        + [
            dma((4,)), dma((4, NB - 1)), dma((4, NB - 1)),
            dma((3, SIDE)), dma((3, SIDE)), dma((3, SIDE)), dma((3, SIDE)),
            dma((3,)), dma((3,)), dma((3,)), dma((3,)),
        ],
        compiler_params=pltpu.CompilerParams(
            collective_id=1, has_side_effects=True, vmem_limit_bytes=VMEM_LIMIT
        ),
    )(fetch_slots, attn, dq, dkg, dkt, dvg, dvt, w_qkv, w_out)


def solution(mesh):
    rows = P(("cluster", "head"), None)
    in_specs = (rows, rows, P(), P(), P("cluster", None), P("cluster"), P())
    return jax.shard_map(
        shards, mesh=mesh, in_specs=in_specs, out_specs=(rows, rows), check_vma=False
    )
```

time: 408 us -> 128 us (0.31)
  waiting for transfers between devices: 203 us -> 0 us
  Pallas kernels: 0 us -> 122 us
  local copies, waits for them, and re-layouts: 83.9 us -> 4.88 us
  blocking collectives: 41.5 us -> 0 us
  other arithmetic: 34.8 us -> 0 us
  matrix products: 27.7 us -> 0 us
  between operations: 14.9 us -> 0.65 us
    unnamed x3 -> x0, waiting for transfers between devices: 135 us -> none
    pallas_call x0 -> x3, Pallas kernels: none -> 122 us  [the longest x1 51.5 us: shards(): pl.pallas_call(forward_kernel, out_shape=[own, own] + ([own] * 4 + [far]...]
    all_gather x1 -> x0, waiting for transfers between devices: 68.1 us -> none  [shards(): kv_table = lax.all_gather(key_value, 'cluster', axis=0, tiled=True)]
    all_to_all x2 -> x0, blocking collectives: 41.5 us -> none  [the longest x1 21.2 us: shards(): lax.all_to_all(packed, 'head', split_axis=2, concat_axis=0, tiled=True)]
    while x33 -> x0, local copies, waits for them, and re-layouts: 31 us -> none  [the longest x1 23.1 us: shards(): lax.map(group_work, (grouped(queries), grouped(grad_heads), grouped(pick_...]
    dot_general x16 -> x0, matrix products: 27.7 us -> none  [the longest x1 5.7 us: shards(): lax.dot_general(restored[:, model_width:], w_qkv, (((1,), (1,)), ((), ())...]
    reshape x3 -> x0, local copies, waits for them, and re-layouts: 20.3 us -> none  [the longest x1 18.4 us: shards(): block_grads = block_grads.reshape(own_blocks * kept_width, feature_size)]
    scatter-add x1 -> x0, other arithmetic: 19.3 us -> none  [shards(): everything = jnp.zeros((own_blocks * cluster_count, feature_size), jnp.fl...]
  transfers between devices with their start and end apart: 2 -> 0, of which waited for: 2 -> 0; matrix products, arithmetic and copies ran while one was open for 2% -> 0% of each run, Pallas kernels for 0% -> 0%
where the time goes in v1:
time: 128 us
  Pallas kernels  122 us (95%)
  local copies, waits for them, and re-layouts  4.88 us (4%)
    pallas_call x1, Pallas kernels, shards(): pl.pallas_call(forward_kernel, out_shape=[own, own] + ([own] * 4 + [far]...  51.5 us
    pallas_call x1, Pallas kernels, shards(): pl.pallas_call(backward_kernel, out_shape=[jax.ShapeDtypeStruct((rows, wi...  46.7 us
    pallas_call x1, Pallas kernels, shards(): pl.pallas_call(attention_kernel, out_shape=[own, own, wide, slim, wide, s...  24 us
    unnamed x3, local copies, waits for them, and re-layouts  4.88 us

profile of v1, /device:TPU:1, one launch (start us, length us, event | category | flops | bytes accessed | tf_op | source)
XLA Modules:
  0.0 127.7 jit_solution(3555631959943804572)
XLA Ops:
  0.6 1.5 %copy.11.fetch = s32[16,16,3]{2,1,0:T(8,128)} copy(s32[16,16,3]{1,0,2:T(8,128)} %param.13) | data formatting | bytes 6144 | tf_op args[6]
  2.2 51.5 %shard_map.86 = (bf16[8,128,128]{2,1,0:T(8,128)(2,1)}, bf16[8,128,128]{2,1,0:T(8,128)(2,1)}, bf16[8,128,128]{2,1,0:T(8,128)(2,1)}, bf16[8,128,128]{2,1,0:T(8,128...) custom-call(bf16[128,1024]{1,0:T(8,128)(2,1)} %feat.1, ...), custom_call_target="tpu_custom_call" | custom-call | tf_op jit(solution)/shard_map/pallas_call | solution.py:485
  53.7 24.0 %shard_map.87 = (bf16[8,128,128]{2,1,0:T(8,128)(2,1)}, bf16[8,128,128]{2,1,0:T(8,128)(2,1)}, f32[32,128,128]{2,1,0:T(8,128)}, bf16[36,128,128]{2,1,0:T(8,128)(2,...) custom-call(s32[8,8]{1,0:T(8,128)} %kept.1, s32[8]{0:T(128)} %count.1, s32[16,16,3]{2,1,0:T(8,128)} %copy.11.fetch, ...), custom_call_target="tpu_custom_call" | custom-call | tf_op jit(solution)/shard_map/pallas_call | solution.py:507
  77.7 46.7 %shard_map.88 = (bf16[128,1024]{1,0:T(8,128)(2,1)}, bf16[128,1024]{1,0:T(8,128)(2,1)}) custom-call(s32[16,16,3]{2,1,0:T(8,128)} %copy.11.fetch, bf16[8,128,128]{2,1,0:T(8,128)(2,1)} %get-tuple-element.40.attn, bf16[8,128,128]{2,1,0:T(8,128)(2,1)} %get-tuple-element.41.dq, f32[32,128,128]{2,1,0:T(8,128)} %get-tuple-element.42.dkg, ...), custom_call_target="tpu_custom_call" | custom-call | tf_op jit(solution)/shard_map/pallas_call | solution.py:523
  124.4 1.7 %copy.14 = bf16[128,1024]{1,0:T(8,128)(2,1)} copy(bf16[128,1024]{1,0:T(8,128)(2,1)} %get-tuple-element.48) | data formatting | bytes 524288
  126.1 1.7 %copy.15 = bf16[128,1024]{1,0:T(8,128)(2,1)} copy(bf16[128,1024]{1,0:T(8,128)(2,1)} %get-tuple-element.49) | data formatting | bytes 524288

commit v2 on v0

v2 whole, which is shorter than its diff:
```python
import jax
import jax.numpy as jnp
from jax import lax
from jax.experimental import pallas as pl
from jax.experimental.pallas import tpu as pltpu
from jax.sharding import PartitionSpec as P

MESH = pl.DeviceIdType.MESH
BF = jnp.bfloat16
F32 = jnp.float32
BLK = 128
HD = 64
NB = 8
SIDE = 4
SLOT = 3
TABLE = NB + SIDE * SIDE * SLOT
LIVE = NB * NB
NEAR = (1, 3, 2)
OUTWARD = (2, 1, 3, 0)
VMEM_LIMIT = 56 << 20

NN = (((1,), (0,)), ((), ()))
NT = (((1,), (1,)), ((), ()))


def dot(a, b, dims=NN):
    return lax.dot_general(a, b, dims, preferred_element_type=F32)


def back_by(d):
    return (SIDE - d) % SIDE


def base(part, d, e):
    return NB + ((e * SIDE + d) if part == 0 else (d * SIDE + e)) * SLOT


def sublayer_kernel(refs):
    feat, gout, wqkv, wout = refs["feat"], refs["gout"], refs["wqkv"], refs["wout"]
    code, count, inverse, fetch = refs["code"], refs["count"], refs["inverse"], refs["fetch"]
    first, table, stage = refs["first"], refs["table"], refs["stage"]
    terms, slot_out, got = refs["terms"], refs["slot_out"], refs["got"]
    own_sum, back_out, back_in = refs["own_sum"], refs["back_out"], refs["back_in"]
    final = refs["final"]
    c = lax.axis_index("cluster")
    h = lax.axis_index("head")
    x, z = c // SIDE, c % SIDE

    def at(part, a, b):
        if part == 1:
            a, b = b, a
        return lax.rem(x + a, SIDE) * SIDE + lax.rem(z + b, SIDE)

    loads = []
    for n, piece in enumerate((1, 2, 0)):
        loads.append(
            pltpu.make_async_copy(
                wqkv.at[:, pl.ds(piece * 1024, 1024)], refs["w"][n], refs["w_sem"].at[n]
            )
        )
    loads.append(pltpu.make_async_copy(wout, refs["w"][3], refs["w_sem"].at[3]))
    for load in loads:
        load.start()

    barrier = pltpu.get_barrier_semaphore()
    for d in (1, 2, 3):
        for part in range(2):
            pl.semaphore_signal(
                barrier, inc=1, device_id=(at(part, d, 0), h), device_id_type=MESH
            )
    for d in range(1, NB):
        pl.semaphore_signal(
            barrier, inc=1, device_id=(c, lax.rem(h + d, NB)), device_id_type=MESH
        )

    pending = []

    def remote(src, dst, send, recv, device):
        return pltpu.make_async_remote_copy(
            src, dst, send, recv, device_id=device, device_id_type=MESH
        )

    def y_copy(kind, src, dst, peer, d):
        return remote(
            src, dst, refs["y_send"].at[kind, d - 1], refs["y_recv"].at[kind, d - 1], (c, peer)
        )

    def y_start(kind, src, dest):
        for d in range(1, NB):
            to = lax.rem(h + d, NB)
            y_copy(kind, src.at[to], dest.at[h], to, d).start()
            pending.append(lambda to=to, d=d: y_copy(kind, src.at[to], dest.at[h], to, d))
        dest[h] = src[h]

    def y_wait(kind, src, dest):
        for d in range(1, NB):
            frm = lax.rem(h - d + NB, NB)
            y_copy(kind, src.at[frm], dest.at[frm], frm, d).wait_recv()

    def project(rows, weight, dims, put):
        for p in range(4):
            if dims is NN:
                w = weight[:, p * 256 : (p + 1) * 256]
            else:
                w = weight[p * 256 : (p + 1) * 256, :]
            out = dot(rows[...], w, dims)
            put(2 * p, out[:, :BLK].T.astype(BF))
            put(2 * p + 1, out[:, BLK:].T.astype(BF))

    def put_heads(part):
        def put(dest, tile):
            refs["y_out"][part][0][dest] = tile[:HD]
            refs["y_out"][part][1][dest] = tile[HD:]

        return put

    def put_whole(n):
        def put(dest, tile):
            refs["qg_out"][n][dest] = tile

        return put

    loads[0].wait()
    project(feat, refs["w"][0], NN, put_heads(0))
    pl.semaphore_wait(barrier, 6 + NB - 1)
    y_start(0, refs["y_out"][0][0], first[0][0][0])
    loads[1].wait()
    project(feat, refs["w"][1], NN, put_heads(1))
    y_start(2, refs["y_out"][1][0], first[1][0][0])
    y_start(1, refs["y_out"][0][1], first[0][1][0])
    y_start(3, refs["y_out"][1][1], first[1][1][0])
    loads[2].wait()
    project(feat, refs["w"][2], NN, put_whole(0))
    y_start(4, refs["qg_out"][0], refs["qg"][0])
    loads[3].wait()
    project(gout, refs["w"][3], NT, put_whole(1))
    y_start(5, refs["qg_out"][1], refs["qg"][1])

    def spread_copy(hh, part, e):
        return remote(
            first[part][hh][0], first[part][hh][e],
            refs["f_send"].at[hh, part, e - 1], refs["f_recv"].at[hh, part, e - 1],
            (at(part, back_by(e), 0), h),
        )

    def pick_copy(hh, part, d, e):
        return remote(
            stage[part][hh].at[d - 1, e],
            table[part][hh].at[pl.ds(base(part, d, e), SLOT)],
            refs["s_send"].at[hh, part, d - 1, e], refs["s_recv"].at[hh, part, d - 1, e],
            (at(part, 0, back_by(d)), h),
        )

    def pick(hh, part, e):
        source = at(part, e, 0)
        for d in NEAR:
            reader = at(part, 0, back_by(d))
            for r in range(SLOT):
                stage[part][hh][d - 1, e, r] = first[part][hh][e][fetch[r, reader, source]]
            pick_copy(hh, part, d, e).start()
            pending.append(lambda d=d: pick_copy(hh, part, d, e))

    def keep(hh, part, e):
        if e == 0:
            for t in range(NB):
                table[part][hh][t] = first[part][hh][0][t]
        else:
            source = at(part, e, 0)
            for r in range(SLOT):
                table[part][hh][base(part, 0, e) + r] = first[part][hh][e][fetch[r, c, source]]

    def forward_start(hh):
        for part in range(2):
            y_wait(2 * part + hh, refs["y_out"][part][hh], first[part][hh][0])
            for e in NEAR:
                spread_copy(hh, part, e).start()
                pending.append(lambda part=part, e=e: spread_copy(hh, part, e))
            pick(hh, part, 0)
        for part in range(2):
            keep(hh, part, 0)

    def forward_step(hh, e):
        for part in range(2):
            spread_copy(hh, part, e).wait_recv()
            pick(hh, part, e)
            keep(hh, part, e)

    def forward_done(hh):
        for part in range(2):
            for e in range(SIDE):
                for d in NEAR:
                    pick_copy(hh, part, d, e).wait_recv()

    def attention(hh, hooks):
        half = slice(hh * HD, (hh + 1) * HD)

        def block(b, _):
            for when, hook in hooks.items():
                pl.when(b == when)(hook)
            n = count[b]
            slots = [code[b, j] for j in range(NB)]
            kc = jnp.concatenate([table[0][hh][i] for i in slots], axis=1)
            vc = jnp.concatenate([table[1][hh][i] for i in slots], axis=1)
            q_t = refs["qg"][0][b, half, :].astype(F32) * 0.125
            g_t = refs["qg"][1][b, half, :].astype(F32)
            q = q_t.T.astype(BF)
            g32 = g_t.T
            g = g32.astype(BF)
            s = dot(q, kc)
            s = jnp.concatenate(
                [jnp.where(j < n, s[:, j * BLK : (j + 1) * BLK], -jnp.inf) for j in range(NB)],
                axis=1,
            )
            p = jnp.exp(s - jnp.max(s, axis=1, keepdims=True))
            a = p * (1.0 / jnp.sum(p, axis=1, keepdims=True))
            low = a.astype(BF)
            attn = dot(low, vc, NT).astype(BF)
            delta = jnp.sum(g32 * attn.astype(F32), axis=1, keepdims=True)
            ds = (a * (dot(g, vc) - delta)).astype(BF)
            dq = (dot(ds, kc, NT) * 0.125).astype(BF)
            dk_t = dot(q_t.astype(BF), ds)
            dv_t = dot(g_t.astype(BF), low)
            for j in range(NB):
                cols = slice(j * BLK, (j + 1) * BLK)
                terms[0][b * NB + j] = dk_t[:, cols]
                terms[1][b * NB + j] = dv_t[:, cols]
            if hh == 0:
                refs["half"][0][b] = attn
                refs["half"][1][b] = dq
            else:
                refs["row_out"][0][b] = jnp.concatenate([refs["half"][0][b], attn], axis=1)
                refs["row_out"][1][b] = jnp.concatenate([refs["half"][1][b], dq], axis=1)
            return 0

        lax.fori_loop(0, NB, block, 0)

    def slot_total(part, slot):
        acc = terms[part][inverse[slot * NB]]
        for b in range(1, NB):
            acc = acc + terms[part][inverse[slot * NB + b]]
        return acc

    def slot_copy(hh, part, d, e):
        return remote(
            slot_out[part][hh].at[d - 1, e],
            got[part][hh][e].at[pl.ds((d - 1) * SLOT, SLOT)],
            refs["g_send"].at[hh, part, d - 1, e], refs["g_recv"].at[hh, part, d - 1, e],
            (at(part, 0, d), h),
        )

    def backward_start(hh):
        for e in OUTWARD:
            for d in NEAR:
                for part in range(2):

                    def one(r, _, e=e, d=d, part=part):
                        total = slot_total(part, base(part, d, e) + r)
                        slot_out[part][hh][d - 1, e, r] = total.astype(BF)
                        return 0

                    lax.fori_loop(0, SLOT, one, 0)
                    slot_copy(hh, part, d, e).start()
                    pending.append(lambda part=part, d=d, e=e: slot_copy(hh, part, d, e))
        for part in range(2):
            for e in (1, 2, 3):

                def near(r, _, e=e, part=part):
                    total = slot_total(part, base(part, 0, e) + r)
                    got[part][hh][e][9 + r] = total.astype(BF)
                    return 0

                lax.fori_loop(0, SLOT, near, 0)

            def own(t, _, part=part):
                own_sum[part][hh][t] = slot_total(part, t)
                return 0

            lax.fori_loop(0, NB, own, 0)

    def back_copy(hh, part, e):
        return remote(
            back_out[part][hh].at[e - 1], back_in[part][hh].at[e - 1],
            refs["b_send"].at[hh, part, e - 1], refs["b_recv"].at[hh, part, e - 1],
            (at(part, e, 0), h),
        )

    def backward_step(hh, e):
        for part in range(2):
            for d in NEAR:
                slot_copy(hh, part, d, e).wait_recv()
            source = at(part, e, 0)

            def one(t, _, part=part, source=source):
                acc = own_sum[part][hh][t] if e == 0 else None
                for d in (0, 1, 2, 3):
                    if d == 0 and e == 0:
                        continue
                    reader = at(part, 0, back_by(d))
                    place = 12
                    for r in range(SLOT):
                        here = (9 if d == 0 else (d - 1) * SLOT) + r
                        place = jnp.where(fetch[r, reader, source] == t, here, place)
                    term = got[part][hh][e][place].astype(F32)
                    acc = term if acc is None else acc + term
                if e == 0:
                    own_sum[part][hh][t] = acc
                else:
                    back_out[part][hh][e - 1, t] = acc.astype(BF)
                return 0

            lax.fori_loop(0, NB, one, 0)
            if e:
                back_copy(hh, part, e).start()
                pending.append(lambda part=part: back_copy(hh, part, e))

    def backward_finish(hh):
        for part in range(2):
            for e in (1, 2, 3):
                back_copy(hh, part, e).wait_recv()

            def one(t, _, part=part):
                acc = own_sum[part][hh][t]
                for e in range(3):
                    acc = acc + back_in[part][hh][e, t].astype(F32)
                final[part][hh][t] = acc.astype(BF)
                return 0

            lax.fori_loop(0, NB, one, 0)
            y_start(8 + 2 * part + hh, final[part][hh], refs["grads"][part][hh])

    forward_start(0)
    for e in NEAR:
        forward_step(0, e)
    forward_start(1)
    for part in range(2):
        terms[part][LIVE] = jnp.zeros((HD, BLK), F32)
        for hh in range(2):
            for e in range(SIDE):
                got[part][hh][e][12] = jnp.zeros((HD, BLK), BF)
    y_wait(4, refs["qg_out"][0], refs["qg"][0])
    y_wait(5, refs["qg_out"][1], refs["qg"][1])
    forward_done(0)
    attention(0, {n + 1: (lambda e=e: forward_step(1, e)) for n, e in enumerate(NEAR)})
    backward_start(0)
    forward_done(1)
    attention(1, {n + 2: (lambda e=e: backward_step(0, e)) for n, e in enumerate(OUTWARD)})
    backward_start(1)
    y_start(6, refs["row_out"][0], refs["rows"][0])
    y_start(7, refs["row_out"][1], refs["rows"][1])
    backward_finish(0)

    def wide(ref):
        return jnp.concatenate([ref[i] for i in range(NB)], axis=1)

    def wide_t(part):
        tiles = []
        for i in range(NB):
            tile = jnp.concatenate([refs["grads"][part][hh][i] for hh in range(2)], axis=0)
            tiles.append(tile.astype(F32).T.astype(BF))
        return jnp.concatenate(tiles, axis=1)

    y_wait(6, refs["row_out"][0], refs["rows"][0])
    refs["attended"][...] = dot(wide(refs["rows"][0]), refs["w"][3][...]).astype(BF)
    y_wait(7, refs["row_out"][1], refs["rows"][1])
    refs["grad"][...] = dot(wide(refs["rows"][1]), refs["w"][2][...], NT)
    for e in OUTWARD:
        backward_step(1, e)
    backward_finish(1)
    for part in range(2):
        for hh in range(2):
            y_wait(8 + 2 * part + hh, final[part][hh], refs["grads"][part][hh])
        term = dot(wide_t(part), refs["w"][part][...], NT)
        if part == 0:
            refs["grad"][...] += term
        else:
            refs["grad_features"][...] = (refs["grad"][...] + term).astype(BF)
    for copy in pending:
        copy().wait_send()


def tree_call(layout, kernel):
    flat, tree = jax.tree.flatten(layout, is_leaf=lambda leaf: not isinstance(leaf, (list, dict)))

    def called(names, *refs):
        kernel({**names, **jax.tree.unflatten(tree, refs)})

    return flat, called


def shards(features, grad_out, w_qkv, w_out, kept_slot, kept_count, fetch_slots):
    dma = pltpu.SemaphoreType.DMA
    c = lax.axis_index("cluster")
    x, z = c // SIDE, c % SIDE
    fetched = jnp.maximum(kept_slot - NB, 0)
    source = fetched // SLOT
    e = (source // SIDE - x + SIDE) % SIDE
    f = (source % SIDE - z + SIDE) % SIDE
    relative = NB + (e * SIDE + f) * SLOT + fetched % SLOT
    code = jnp.where(kept_slot < NB, kept_slot, relative)
    entry = jnp.arange(NB, dtype=jnp.int32)
    live = entry[None, :] < kept_count[:, None]
    code = jnp.where(live, code, entry[:, None])
    slots = jnp.arange(TABLE, dtype=jnp.int32)
    hits = (code[None] == slots[:, None, None]) & live[None]
    spot = entry[:, None] * NB + entry[None, :]
    inverse = jnp.min(jnp.where(hits, spot[None], LIVE), axis=2).reshape(-1)

    def vm(*shape, dtype=BF):
        return pltpu.VMEM(shape, dtype)

    def each(make, *counts):
        if not counts:
            return make()
        return [each(make, *counts[1:]) for _ in range(counts[0])]

    tile = (HD, BLK)
    layout = {
        "w": each(lambda: vm(1024, 1024), 4),
        "y_out": each(lambda: vm(NB, *tile), 2, 2),
        "qg_out": each(lambda: vm(NB, BLK, BLK), 2),
        "qg": each(lambda: vm(NB, BLK, BLK), 2),
        "first": each(lambda: vm(NB, *tile), 2, 2, SIDE),
        "table": each(lambda: vm(TABLE, *tile), 2, 2),
        "stage": each(lambda: vm(3, SIDE, SLOT, *tile), 2, 2),
        "terms": each(lambda: vm(LIVE + 1, *tile, dtype=F32), 2),
        "half": each(lambda: vm(NB, BLK, HD), 2),
        "row_out": each(lambda: vm(NB, BLK, BLK), 2),
        "rows": each(lambda: vm(NB, BLK, BLK), 2),
        "slot_out": each(lambda: vm(3, SIDE, SLOT, *tile), 2, 2),
        "got": each(lambda: vm(13, *tile), 2, 2, SIDE),
        "own_sum": each(lambda: vm(NB, *tile, dtype=F32), 2, 2),
        "back_out": each(lambda: vm(3, NB, *tile), 2, 2),
        "back_in": each(lambda: vm(3, NB, *tile), 2, 2),
        "final": each(lambda: vm(NB, *tile), 2, 2),
        "grads": each(lambda: vm(NB, *tile), 2, 2),
        "grad": vm(BLK, 1024, dtype=F32),
        "w_sem": dma((4,)),
        "y_send": dma((12, NB - 1)),
        "y_recv": dma((12, NB - 1)),
        "f_send": dma((2, 2, 3)),
        "f_recv": dma((2, 2, 3)),
        "s_send": dma((2, 2, 3, SIDE)),
        "s_recv": dma((2, 2, 3, SIDE)),
        "g_send": dma((2, 2, 3, SIDE)),
        "g_recv": dma((2, 2, 3, SIDE)),
        "b_send": dma((2, 2, 3)),
        "b_recv": dma((2, 2, 3)),
    }
    scratch, called = tree_call(layout, sublayer_kernel)
    names = ("feat", "gout", "wqkv", "wout", "code", "count", "inverse", "fetch")
    names += ("attended", "grad_features")

    def kernel(*refs):
        called(dict(zip(names, refs)), *refs[len(names) :])

    spec = pl.BlockSpec
    near = spec(memory_space=pltpu.VMEM)
    far = spec(memory_space=pl.ANY)
    scalars = spec(memory_space=pltpu.SMEM)
    return pl.pallas_call(
        kernel,
        out_shape=[jax.ShapeDtypeStruct(features.shape, BF)] * 2,
        in_specs=[near, near, far, far, scalars, scalars, scalars, scalars],
        out_specs=[near, near],
        scratch_shapes=scratch,
        compiler_params=pltpu.CompilerParams(
            collective_id=0, has_side_effects=True, vmem_limit_bytes=VMEM_LIMIT
        ),
    )(
        features, grad_out, w_qkv, w_out, code, kept_count, inverse,
        jnp.transpose(fetch_slots, (2, 0, 1)),
    )


def solution(mesh):
    rows = P(("cluster", "head"), None)
    in_specs = (rows, rows, P(), P(), P("cluster", None), P("cluster"), P())
    return jax.shard_map(
        shards, mesh=mesh, in_specs=in_specs, out_specs=(rows, rows), check_vma=False
    )
```

time: 408 us -> 96.4 us (0.24)
  waiting for transfers between devices: 203 us -> 0 us
  Pallas kernels: 0 us -> 89.8 us
  local copies, waits for them, and re-layouts: 83.9 us -> 4.09 us
  blocking collectives: 41.5 us -> 0 us
  other arithmetic: 34.8 us -> 1.59 us
  matrix products: 27.7 us -> 0 us
  between operations: 14.9 us -> 0.68 us
    unnamed x3 -> x0, waiting for transfers between devices: 135 us -> none
    pallas_call x0 -> x1, Pallas kernels: none -> 89.8 us  [shards(): pl.pallas_call(kernel, out_shape=[jax.ShapeDtypeStruct(features.shape, BF...]
    all_gather x1 -> x0, waiting for transfers between devices: 68.1 us -> none  [shards(): kv_table = lax.all_gather(key_value, 'cluster', axis=0, tiled=True)]
    all_to_all x2 -> x0, blocking collectives: 41.5 us -> none  [the longest x1 21.2 us: shards(): lax.all_to_all(packed, 'head', split_axis=2, concat_axis=0, tiled=True)]
    while x33 -> x0, local copies, waits for them, and re-layouts: 31 us -> none  [the longest x1 23.1 us: shards(): lax.map(group_work, (grouped(queries), grouped(grad_heads), grouped(pick_...]
    dot_general x16 -> x0, matrix products: 27.7 us -> none  [the longest x1 5.7 us: shards(): lax.dot_general(restored[:, model_width:], w_qkv, (((1,), (1,)), ((), ())...]
    reshape x3 -> x1, local copies, waits for them, and re-layouts: 20.3 us -> 0.67 us  [shards(): inverse = jnp.min(jnp.where(hits, spot[None], LIVE), axis=2).reshape(-1)]
    scatter-add x1 -> x0, other arithmetic: 19.3 us -> none  [shards(): everything = jnp.zeros((own_blocks * cluster_count, feature_size), jnp.fl...]
  transfers between devices with their start and end apart: 2 -> 0, of which waited for: 2 -> 0; matrix products, arithmetic and copies ran while one was open for 2% -> 0% of each run, Pallas kernels for 0% -> 0%
where the time goes in v2:
time: 96.4 us; the launch traced here: 96.1 us
  Pallas kernels  89.8 us (93%)
  local copies, waits for them, and re-layouts  4.09 us (4%)
  other arithmetic  1.59 us (2%)
    pallas_call x1, Pallas kernels, shards(): pl.pallas_call(kernel, out_shape=[jax.ShapeDtypeStruct(features.shape, BF...  89.8 us
    unnamed x4, local copies, waits for them, and re-layouts  3.34 us

profile of v2, /device:TPU:1, one launch (start us, length us, event | category | flops | bytes accessed | tf_op | source)
XLA Modules:
  0.0 96.1 jit_solution(10144160661574591140)
XLA Ops:
  0.7 0.7 iota_compare_fusion.1
  1.4 0.8 fusion.12
  2.2 0.0 copy-start
  2.2 0.1 select_reduce_fusion
  2.3 0.1 copy.9
  2.3 0.7 reshape.49.refs_6_
  3.0 0.0 copy-done
  3.0 89.8 %shard_map.86 = (bf16[128,1024]{1,0:T(8,128)(2,1)}, bf16[128,1024]{1,0:T(8,128)(2,1)}) custom-call(bf16[128,1024]{1,0:T(8,128)(2,1)} %refs_0_.1, bf16[128,1024]{1,0:T(8,128)(2,1)} %refs_1_.1, bf16[1024,3072]{1,0:T(8,128)(2,1)} %refs_2_.1, bf16[1024,1024]{1,0:T(8,128)(2,1)} %refs_3_.1, s32[8,8]{1,0:T(8,128)} %copy-done, s32[8]{0:T(128)} %refs_5_.1, ...), custom_call_target="tpu_custom_call" | custom-call | tf_op jit(solution)/shard_map/pallas_call | solution.py:460
  92.8 1.7 %copy.12 = bf16[128,1024]{1,0:T(8,128)(2,1)} copy(bf16[128,1024]{1,0:T(8,128)(2,1)} %get-tuple-element.6) | data formatting | bytes 524288
  94.5 1.7 %copy.13 = bf16[128,1024]{1,0:T(8,128)(2,1)} copy(bf16[128,1024]{1,0:T(8,128)(2,1)} %get-tuple-element.7) | data formatting | bytes 524288
  (1 shorter events, 0.0 us)
Async XLA Ops:
  2.2 0.9 copy-start

commit v3 on v2

--- a/solution.py
+++ b/solution.py
@@ -37,7 +37,7 @@
 
 def sublayer_kernel(refs):
     feat, gout, wqkv, wout = refs["feat"], refs["gout"], refs["wqkv"], refs["wout"]
-    code, count, inverse, fetch = refs["code"], refs["count"], refs["inverse"], refs["fetch"]
+    index, count, fetch = refs["index"], refs["count"], refs["fetch"]
     first, table, stage = refs["first"], refs["table"], refs["stage"]
     terms, slot_out, got = refs["terms"], refs["slot_out"], refs["got"]
     own_sum, back_out, back_in = refs["own_sum"], refs["back_out"], refs["back_in"]
@@ -51,16 +51,17 @@
             a, b = b, a
         return lax.rem(x + a, SIDE) * SIDE + lax.rem(z + b, SIDE)
 
-    loads = []
+    def load(n, src, dst):
+        return pltpu.make_async_copy(src, dst, refs["w_sem"].at[n])
+
+    loads = [load(4, refs["feat_in"], feat), load(5, refs["gout_in"], gout)]
     for n, piece in enumerate((1, 2, 0)):
-        loads.append(
-            pltpu.make_async_copy(
-                wqkv.at[:, pl.ds(piece * 1024, 1024)], refs["w"][n], refs["w_sem"].at[n]
-            )
-        )
-    loads.append(pltpu.make_async_copy(wout, refs["w"][3], refs["w_sem"].at[3]))
-    for load in loads:
-        load.start()
+        loads.append(load(n, wqkv.at[:, pl.ds(piece * 1024, 1024)], refs["w"][n]))
+    loads.append(load(3, wout, refs["w"][3]))
+    load_feat, load_gout, load_k, load_v, load_q, load_o = loads
+    load_feat.start()
+    load_k.start()
+    load_v.start()
 
     barrier = pltpu.get_barrier_semaphore()
     for d in (1, 2, 3):
@@ -73,29 +74,26 @@
             barrier, inc=1, device_id=(c, lax.rem(h + d, NB)), device_id_type=MESH
         )
 
-    pending = []
-
     def remote(src, dst, send, recv, device):
         return pltpu.make_async_remote_copy(
             src, dst, send, recv, device_id=device, device_id_type=MESH
         )
 
-    def y_copy(kind, src, dst, peer, d):
-        return remote(
-            src, dst, refs["y_send"].at[kind, d - 1], refs["y_recv"].at[kind, d - 1], (c, peer)
-        )
+    def y_copy(kind, src, dst, peer):
+        return remote(src, dst, refs["y_send"].at[kind], refs["y_recv"].at[kind], (c, peer))
 
     def y_start(kind, src, dest):
         for d in range(1, NB):
             to = lax.rem(h + d, NB)
-            y_copy(kind, src.at[to], dest.at[h], to, d).start()
-            pending.append(lambda to=to, d=d: y_copy(kind, src.at[to], dest.at[h], to, d))
+            y_copy(kind, src.at[to], dest.at[h], to).start()
         dest[h] = src[h]
 
+    def y_all(kind, src, dest):
+        others = pl.ds(0, NB - 1)
+        return y_copy(kind, src.at[others], dest.at[others], lax.rem(h + 1, NB))
+
     def y_wait(kind, src, dest):
-        for d in range(1, NB):
-            frm = lax.rem(h - d + NB, NB)
-            y_copy(kind, src.at[frm], dest.at[frm], frm, d).wait_recv()
+        y_all(kind, src, dest).wait_recv()
 
     def project(rows, weight, dims, put):
         for p in range(4):
@@ -120,34 +118,71 @@
 
         return put
 
-    loads[0].wait()
+    def index_tables():
+        kept = refs["kept"][...]
+        fetched = jnp.maximum(kept - NB, 0)
+        source = (fetched * 43) >> 7
+        e = ((source >> 2) - x + SIDE) & 3
+        f = ((source & 3) - z + SIDE) & 3
+        relative = NB + (e * SIDE + f) * SLOT + fetched - source * SLOT
+        slots = jnp.where(kept < NB, kept, relative)
+        row = lax.broadcasted_iota(jnp.int32, (NB, NB), 0)
+        limit = jnp.zeros((NB, NB), jnp.int32)
+        for b in range(NB):
+            limit = jnp.where(row == b, count[b], limit)
+        column = lax.broadcasted_iota(jnp.int32, (NB, NB), 1)
+        slots = jnp.where(column < limit, slots, row)
+        lane = lax.broadcasted_iota(jnp.int32, (NB, BLK), 1)
+        wide_row = lax.broadcasted_iota(jnp.int32, (NB, BLK), 0)
+        entry_of = jnp.full((NB, BLK), LIVE, jnp.int32)
+        for j in range(NB):
+            hit = (slots[:, j : j + 1] == lane) & (limit[:, j : j + 1] > j)
+            entry_of = jnp.where(hit, wide_row * NB + j, entry_of)
+        refs["index_v"][0:NB] = jnp.zeros((NB, BLK), jnp.int32)
+        refs["index_v"][0:NB, 0:NB] = slots
+        refs["index_v"][NB : 2 * NB] = entry_of
+        copy = load(6, refs["index_v"], index)
+        copy.start()
+        return copy
+
+    index_copy = index_tables()
+    load_feat.wait()
+    load_k.wait()
     project(feat, refs["w"][0], NN, put_heads(0))
     pl.semaphore_wait(barrier, 6 + NB - 1)
     y_start(0, refs["y_out"][0][0], first[0][0][0])
-    loads[1].wait()
+    load_gout.start()
+    load_q.start()
+    load_o.start()
+    load_v.wait()
     project(feat, refs["w"][1], NN, put_heads(1))
     y_start(2, refs["y_out"][1][0], first[1][0][0])
     y_start(1, refs["y_out"][0][1], first[0][1][0])
     y_start(3, refs["y_out"][1][1], first[1][1][0])
-    loads[2].wait()
+    load_q.wait()
     project(feat, refs["w"][2], NN, put_whole(0))
     y_start(4, refs["qg_out"][0], refs["qg"][0])
-    loads[3].wait()
+    load_gout.wait()
+    load_o.wait()
     project(gout, refs["w"][3], NT, put_whole(1))
     y_start(5, refs["qg_out"][1], refs["qg"][1])
-
-    def spread_copy(hh, part, e):
+    index_copy.wait()
+
+    def spread_copy(hh, part, src, e, blocks, to):
         return remote(
-            first[part][hh][0], first[part][hh][e],
-            refs["f_send"].at[hh, part, e - 1], refs["f_recv"].at[hh, part, e - 1],
-            (at(part, back_by(e), 0), h),
+            first[part][hh][src].at[blocks], first[part][hh][e].at[blocks],
+            refs["f_send"].at[hh, part], refs["f_recv"].at[hh, part, e - 1],
+            (at(part, to, 0), h),
         )
+
+    def spread_wait(hh, part, e):
+        spread_copy(hh, part, 0, e, pl.ds(0, NB), e).wait_recv()
 
     def pick_copy(hh, part, d, e):
         return remote(
             stage[part][hh].at[d - 1, e],
             table[part][hh].at[pl.ds(base(part, d, e), SLOT)],
-            refs["s_send"].at[hh, part, d - 1, e], refs["s_recv"].at[hh, part, d - 1, e],
+            refs["s_send"].at[hh, part], refs["s_recv"].at[hh, part],
             (at(part, 0, back_by(d)), h),
         )
 
@@ -158,7 +193,6 @@
             for r in range(SLOT):
                 stage[part][hh][d - 1, e, r] = first[part][hh][e][fetch[r, reader, source]]
             pick_copy(hh, part, d, e).start()
-            pending.append(lambda d=d: pick_copy(hh, part, d, e))
 
     def keep(hh, part, e):
         if e == 0:
@@ -172,24 +206,29 @@
     def forward_start(hh):
         for part in range(2):
             y_wait(2 * part + hh, refs["y_out"][part][hh], first[part][hh][0])
-            for e in NEAR:
-                spread_copy(hh, part, e).start()
-                pending.append(lambda part=part, e=e: spread_copy(hh, part, e))
+            for e in (1, 3):
+                spread_copy(hh, part, 0, e, pl.ds(0, NB), back_by(e)).start()
             pick(hh, part, 0)
         for part in range(2):
             keep(hh, part, 0)
 
     def forward_step(hh, e):
         for part in range(2):
-            spread_copy(hh, part, e).wait_recv()
+            spread_wait(hh, part, e)
+            if e == 1:
+                spread_copy(hh, part, 1, 2, pl.ds(0, NB // 2), 3).start()
+            if e == 3:
+                spread_copy(hh, part, 3, 2, pl.ds(NB // 2, NB // 2), 1).start()
             pick(hh, part, e)
             keep(hh, part, e)
 
+    def stand_in(part, hh, send, recv, blocks):
+        some = table[part][hh].at[pl.ds(0, blocks)]
+        return remote(some, some, send.at[hh, part], recv.at[hh, part], (at(part, 1, 0), h))
+
     def forward_done(hh):
         for part in range(2):
-            for e in range(SIDE):
-                for d in NEAR:
-                    pick_copy(hh, part, d, e).wait_recv()
+            stand_in(part, hh, refs["s_send"], refs["s_recv"], 3 * SIDE * SLOT).wait_recv()
 
     def attention(hh, hooks):
         half = slice(hh * HD, (hh + 1) * HD)
@@ -198,7 +237,7 @@
             for when, hook in hooks.items():
                 pl.when(b == when)(hook)
             n = count[b]
-            slots = [code[b, j] for j in range(NB)]
+            slots = [index[b, j] for j in range(NB)]
             kc = jnp.concatenate([table[0][hh][i] for i in slots], axis=1)
             vc = jnp.concatenate([table[1][hh][i] for i in slots], axis=1)
             q_t = refs["qg"][0][b, half, :].astype(F32) * 0.125
@@ -235,16 +274,16 @@
         lax.fori_loop(0, NB, block, 0)
 
     def slot_total(part, slot):
-        acc = terms[part][inverse[slot * NB]]
+        acc = terms[part][index[NB, slot]]
         for b in range(1, NB):
-            acc = acc + terms[part][inverse[slot * NB + b]]
+            acc = acc + terms[part][index[NB + b, slot]]
         return acc
 
     def slot_copy(hh, part, d, e):
         return remote(
             slot_out[part][hh].at[d - 1, e],
             got[part][hh][e].at[pl.ds((d - 1) * SLOT, SLOT)],
-            refs["g_send"].at[hh, part, d - 1, e], refs["g_recv"].at[hh, part, d - 1, e],
+            refs["g_send"].at[hh, part], refs["g_recv"].at[hh, part, e],
             (at(part, 0, d), h),
         )
 
@@ -260,7 +299,6 @@
 
                     lax.fori_loop(0, SLOT, one, 0)
                     slot_copy(hh, part, d, e).start()
-                    pending.append(lambda part=part, d=d, e=e: slot_copy(hh, part, d, e))
         for part in range(2):
             for e in (1, 2, 3):
 
@@ -280,14 +318,17 @@
     def back_copy(hh, part, e):
         return remote(
             back_out[part][hh].at[e - 1], back_in[part][hh].at[e - 1],
-            refs["b_send"].at[hh, part, e - 1], refs["b_recv"].at[hh, part, e - 1],
+            refs["b_send"].at[hh, part], refs["b_recv"].at[hh, part],
             (at(part, e, 0), h),
         )
 
     def backward_step(hh, e):
         for part in range(2):
-            for d in NEAR:
-                slot_copy(hh, part, d, e).wait_recv()
+            some = got[part][hh][e].at[pl.ds(0, 3 * SLOT)]
+            remote(
+                some, some, refs["g_send"].at[hh, part], refs["g_recv"].at[hh, part, e],
+                (at(part, 0, 1), h),
+            ).wait_recv()
             source = at(part, e, 0)
 
             def one(t, _, part=part, source=source):
@@ -311,12 +352,10 @@
             lax.fori_loop(0, NB, one, 0)
             if e:
                 back_copy(hh, part, e).start()
-                pending.append(lambda part=part: back_copy(hh, part, e))
 
     def backward_finish(hh):
         for part in range(2):
-            for e in (1, 2, 3):
-                back_copy(hh, part, e).wait_recv()
+            stand_in(part, hh, refs["b_send"], refs["b_recv"], 3 * NB).wait_recv()
 
             def one(t, _, part=part):
                 acc = own_sum[part][hh][t]
@@ -360,7 +399,9 @@
         return jnp.concatenate(tiles, axis=1)
 
     y_wait(6, refs["row_out"][0], refs["rows"][0])
-    refs["attended"][...] = dot(wide(refs["rows"][0]), refs["w"][3][...]).astype(BF)
+    refs["att"][...] = dot(wide(refs["rows"][0]), refs["w"][3][...]).astype(BF)
+    save_att = load(0, refs["att"], refs["attended"])
+    save_att.start()
     y_wait(7, refs["row_out"][1], refs["rows"][1])
     refs["grad"][...] = dot(wide(refs["rows"][1]), refs["w"][2][...], NT)
     for e in OUTWARD:
@@ -373,9 +414,24 @@
         if part == 0:
             refs["grad"][...] += term
         else:
-            refs["grad_features"][...] = (refs["grad"][...] + term).astype(BF)
-    for copy in pending:
-        copy().wait_send()
+            refs["gf"][...] = (refs["grad"][...] + term).astype(BF)
+    save_gf = load(1, refs["gf"], refs["grad_features"])
+    save_gf.start()
+    for part in range(2):
+        y_all(4 + part, refs["qg_out"][part], refs["qg"][part]).wait_send()
+        y_all(6 + part, refs["row_out"][part], refs["rows"][part]).wait_send()
+        for hh in range(2):
+            y_all(2 * part + hh, refs["y_out"][part][hh], first[part][hh][0]).wait_send()
+            y_all(8 + 2 * part + hh, final[part][hh], refs["grads"][part][hh]).wait_send()
+            for name, blocks in (("f", 24), ("s", 36), ("g", 36), ("b", 24)):
+                stand_in(part, hh, refs[name + "_send"], refs["s_recv"], blocks).wait_send()
+    save_att.wait()
+    save_gf.wait()
+
+
+def copy_kernel(attended, grad_features, attended_out, grad_features_out):
+    attended_out[...] = attended[...]
+    grad_features_out[...] = grad_features[...]
 
 
 def tree_call(layout, kernel):
@@ -389,22 +445,6 @@
 
 def shards(features, grad_out, w_qkv, w_out, kept_slot, kept_count, fetch_slots):
     dma = pltpu.SemaphoreType.DMA
-    c = lax.axis_index("cluster")
-    x, z = c // SIDE, c % SIDE
-    fetched = jnp.maximum(kept_slot - NB, 0)
-    source = fetched // SLOT
-    e = (source // SIDE - x + SIDE) % SIDE
-    f = (source % SIDE - z + SIDE) % SIDE
-    relative = NB + (e * SIDE + f) * SLOT + fetched % SLOT
-    code = jnp.where(kept_slot < NB, kept_slot, relative)
-    entry = jnp.arange(NB, dtype=jnp.int32)
-    live = entry[None, :] < kept_count[:, None]
-    code = jnp.where(live, code, entry[:, None])
-    slots = jnp.arange(TABLE, dtype=jnp.int32)
-    hits = (code[None] == slots[:, None, None]) & live[None]
-    spot = entry[:, None] * NB + entry[None, :]
-    inverse = jnp.min(jnp.where(hits, spot[None], LIVE), axis=2).reshape(-1)
-
     def vm(*shape, dtype=BF):
         return pltpu.VMEM(shape, dtype)
 
@@ -434,42 +474,51 @@
         "final": each(lambda: vm(NB, *tile), 2, 2),
         "grads": each(lambda: vm(NB, *tile), 2, 2),
         "grad": vm(BLK, 1024, dtype=F32),
-        "w_sem": dma((4,)),
-        "y_send": dma((12, NB - 1)),
-        "y_recv": dma((12, NB - 1)),
-        "f_send": dma((2, 2, 3)),
+        "feat": vm(BLK, 1024),
+        "gout": vm(BLK, 1024),
+        "att": vm(BLK, 1024),
+        "gf": vm(BLK, 1024),
+        "index_v": vm(2 * NB, BLK, dtype=jnp.int32),
+        "index": pltpu.SMEM((2 * NB, BLK), jnp.int32),
+        "w_sem": dma((7,)),
+        "y_send": dma((12,)),
+        "y_recv": dma((12,)),
+        "f_send": dma((2, 2)),
         "f_recv": dma((2, 2, 3)),
-        "s_send": dma((2, 2, 3, SIDE)),
-        "s_recv": dma((2, 2, 3, SIDE)),
-        "g_send": dma((2, 2, 3, SIDE)),
-        "g_recv": dma((2, 2, 3, SIDE)),
-        "b_send": dma((2, 2, 3)),
-        "b_recv": dma((2, 2, 3)),
+        "s_send": dma((2, 2)),
+        "s_recv": dma((2, 2)),
+        "g_send": dma((2, 2)),
+        "g_recv": dma((2, 2, SIDE)),
+        "b_send": dma((2, 2)),
+        "b_recv": dma((2, 2)),
     }
     scratch, called = tree_call(layout, sublayer_kernel)
-    names = ("feat", "gout", "wqkv", "wout", "code", "count", "inverse", "fetch")
+    names = ("feat_in", "gout_in", "wqkv", "wout", "kept", "count", "fetch")
     names += ("attended", "grad_features")
 
     def kernel(*refs):
         called(dict(zip(names, refs)), *refs[len(names) :])
 
-    spec = pl.BlockSpec
-    near = spec(memory_space=pltpu.VMEM)
-    far = spec(memory_space=pl.ANY)
-    scalars = spec(memory_space=pltpu.SMEM)
-    return pl.pallas_call(
+    near = pl.BlockSpec(memory_space=pltpu.VMEM)
+    far = pl.BlockSpec(memory_space=pl.ANY)
+    scalars = pl.BlockSpec(memory_space=pltpu.SMEM)
+    out_shape = [jax.ShapeDtypeStruct(features.shape, BF)] * 2
+    results = pl.pallas_call(
         kernel,
-        out_shape=[jax.ShapeDtypeStruct(features.shape, BF)] * 2,
-        in_specs=[near, near, far, far, scalars, scalars, scalars, scalars],
-        out_specs=[near, near],
+        out_shape=out_shape,
+        in_specs=[far, far, far, far, near, scalars, scalars],
+        out_specs=[far, far],
         scratch_shapes=scratch,
         compiler_params=pltpu.CompilerParams(
             collective_id=0, has_side_effects=True, vmem_limit_bytes=VMEM_LIMIT
         ),
     )(
-        features, grad_out, w_qkv, w_out, code, kept_count, inverse,
+        features, grad_out, w_qkv, w_out, kept_slot, kept_count,
         jnp.transpose(fetch_slots, (2, 0, 1)),
     )
+    return pl.pallas_call(
+        copy_kernel, out_shape=out_shape, in_specs=[near, near], out_specs=[near, near]
+    )(*results)
 
 
 def solution(mesh):

time: 96.4 us -> 92.8 us (0.963)
  local copies, waits for them, and re-layouts: 4.09 us -> 0 us
  Pallas kernels: 89.8 us -> 91.9 us
  other arithmetic: 1.59 us -> 0 us
    unnamed x4 -> x0, local copies, waits for them, and re-layouts: 3.34 us -> none
    pallas_call x1 -> x2, Pallas kernels: 89.8 us -> 91.9 us  [the longest x1 90.1 us: shards(): pl.pallas_call(kernel, out_shape=out_shape, in_specs=[far, far, far, far,...]
where the time goes in v3:
time: 92.8 us; the launch traced here: 92.5 us
  Pallas kernels  91.9 us (99%)
    pallas_call x1, Pallas kernels, shards(): pl.pallas_call(kernel, out_shape=out_shape, in_specs=[far, far, far, far,...  90.1 us

profile of v3, /device:TPU:1, one launch (start us, length us, event | category | flops | bytes accessed | tf_op | source)
XLA Modules:
  0.0 92.5 jit_solution(7303386025405702695)
XLA Ops:
  0.6 90.1 %shard_map.86 = (bf16[128,1024]{1,0:T(8,128)(2,1)}, bf16[128,1024]{1,0:T(8,128)(2,1)}) custom-call(bf16[128,1024]{1,0:T(8,128)(2,1)} %refs_0_.1, bf16[128,1024]{1,0:T(8,128)(2,1)} %refs_1_.1, bf16[1024,3072]{1,0:T(8,128)(2,1)} %refs_2_.1, bf16[1024,1024]{1,0:T(8,128)(2,1)} %refs_3_.1, s32[8,8]{1,0:T(8,128)} %refs_4_.1, s32[8]{0:T(128)} %refs_5_.1, ...), custom_call_target="tpu_custom_call" | custom-call | tf_op jit(solution)/shard_map/pallas_call | solution.py:506
  90.7 1.8 %shard_map.87 = (bf16[128,1024]{1,0:T(8,128)(2,1)}, bf16[128,1024]{1,0:T(8,128)(2,1)}) custom-call(bf16[128,1024]{1,0:T(8,128)(2,1)} %get-tuple-element.4.attended, bf16[128,1024]{1,0:T(8,128)(2,1)} %get-tuple-element.5.grad_features), custom_call_target="tpu_custom_call" | custom-call | tf_op jit(solution)/shard_map/pallas_call | solution.py:519

commit v4 on v3

--- a/solution.py
+++ b/solution.py
@@ -14,6 +14,7 @@
 SIDE = 4
 SLOT = 3
 TABLE = NB + SIDE * SIDE * SLOT
+GROUP = 4
 LIVE = NB * NB
 NEAR = (1, 3, 2)
 OUTWARD = (2, 1, 3, 0)
@@ -230,48 +231,61 @@
         for part in range(2):
             stand_in(part, hh, refs["s_send"], refs["s_recv"], 3 * SIDE * SLOT).wait_recv()
 
-    def attention(hh, hooks):
+    def attention(hh):
         half = slice(hh * HD, (hh + 1) * HD)
 
-        def block(b, _):
-            for when, hook in hooks.items():
-                pl.when(b == when)(hook)
-            n = count[b]
+        def load_block(b):
             slots = [index[b, j] for j in range(NB)]
             kc = jnp.concatenate([table[0][hh][i] for i in slots], axis=1)
             vc = jnp.concatenate([table[1][hh][i] for i in slots], axis=1)
             q_t = refs["qg"][0][b, half, :].astype(F32) * 0.125
             g_t = refs["qg"][1][b, half, :].astype(F32)
-            q = q_t.T.astype(BF)
-            g32 = g_t.T
-            g = g32.astype(BF)
-            s = dot(q, kc)
-            s = jnp.concatenate(
-                [jnp.where(j < n, s[:, j * BLK : (j + 1) * BLK], -jnp.inf) for j in range(NB)],
-                axis=1,
-            )
-            p = jnp.exp(s - jnp.max(s, axis=1, keepdims=True))
-            a = p * (1.0 / jnp.sum(p, axis=1, keepdims=True))
-            low = a.astype(BF)
-            attn = dot(low, vc, NT).astype(BF)
-            delta = jnp.sum(g32 * attn.astype(F32), axis=1, keepdims=True)
-            ds = (a * (dot(g, vc) - delta)).astype(BF)
-            dq = (dot(ds, kc, NT) * 0.125).astype(BF)
-            dk_t = dot(q_t.astype(BF), ds)
-            dv_t = dot(g_t.astype(BF), low)
-            for j in range(NB):
-                cols = slice(j * BLK, (j + 1) * BLK)
-                terms[0][b * NB + j] = dk_t[:, cols]
-                terms[1][b * NB + j] = dv_t[:, cols]
-            if hh == 0:
-                refs["half"][0][b] = attn
-                refs["half"][1][b] = dq
-            else:
-                refs["row_out"][0][b] = jnp.concatenate([refs["half"][0][b], attn], axis=1)
-                refs["row_out"][1][b] = jnp.concatenate([refs["half"][1][b], dq], axis=1)
+            return kc, vc, q_t, g_t
+
+        def block(i, _):
+            blocks = [i * GROUP + n for n in range(GROUP)]
+            loaded = [load_block(b) for b in blocks]
+            scores = []
+            for b, (kc, vc, q_t, g_t) in zip(blocks, loaded):
+                s = dot(q_t.T.astype(BF), kc)
+                n = count[b]
+                scores.append(
+                    jnp.concatenate(
+                        [
+                            jnp.where(j < n, s[:, j * BLK : (j + 1) * BLK], -jnp.inf)
+                            for j in range(NB)
+                        ],
+                        axis=1,
+                    )
+                )
+            probs = []
+            for s in scores:
+                p = jnp.exp(s - jnp.max(s, axis=1, keepdims=True))
+                probs.append(p * (1.0 / jnp.sum(p, axis=1, keepdims=True)))
+            lows = [a.astype(BF) for a in probs]
+            attns = [dot(low, vc, NT).astype(BF) for low, (_, vc, _, _) in zip(lows, loaded)]
+            grads = []
+            for a, attn, (kc, vc, q_t, g_t) in zip(probs, attns, loaded):
+                g = g_t.T
+                delta = jnp.sum(g * attn.astype(F32), axis=1, keepdims=True)
+                grads.append((a * (dot(g.astype(BF), vc) - delta)).astype(BF))
+            for b, low, ds, attn, (kc, vc, q_t, g_t) in zip(blocks, lows, grads, attns, loaded):
+                dq = (dot(ds, kc, NT) * 0.125).astype(BF)
+                dk_t = dot(q_t.astype(BF), ds)
+                dv_t = dot(g_t.astype(BF), low)
+                for j in range(NB):
+                    cols = slice(j * BLK, (j + 1) * BLK)
+                    terms[0][b * NB + j] = dk_t[:, cols]
+                    terms[1][b * NB + j] = dv_t[:, cols]
+                if hh == 0:
+                    refs["half"][0][b] = attn
+                    refs["half"][1][b] = dq
+                else:
+                    refs["row_out"][0][b] = jnp.concatenate([refs["half"][0][b], attn], axis=1)
+                    refs["row_out"][1][b] = jnp.concatenate([refs["half"][1][b], dq], axis=1)
             return 0
 
-        lax.fori_loop(0, NB, block, 0)
+        lax.fori_loop(0, NB // GROUP, block, 0)
 
     def slot_total(part, slot):
         acc = terms[part][index[NB, slot]]
@@ -378,14 +392,19 @@
                 got[part][hh][e][12] = jnp.zeros((HD, BLK), BF)
     y_wait(4, refs["qg_out"][0], refs["qg"][0])
     y_wait(5, refs["qg_out"][1], refs["qg"][1])
+    forward_step(1, 1)
+    forward_step(1, 3)
     forward_done(0)
-    attention(0, {n + 1: (lambda e=e: forward_step(1, e)) for n, e in enumerate(NEAR)})
+    attention(0)
+    forward_step(1, 2)
     backward_start(0)
     forward_done(1)
-    attention(1, {n + 2: (lambda e=e: backward_step(0, e)) for n, e in enumerate(OUTWARD)})
+    attention(1)
     backward_start(1)
     y_start(6, refs["row_out"][0], refs["rows"][0])
     y_start(7, refs["row_out"][1], refs["rows"][1])
+    for e in OUTWARD:
+        backward_step(0, e)
     backward_finish(0)
 
     def wide(ref):

time: 92.8 us -> 85 us (0.916)
  Pallas kernels: 91.9 us -> 84.1 us
    pallas_call x1, Pallas kernels: 90.1 us -> 82.3 us  [shards(): pl.pallas_call(kernel, out_shape=out_shape, in_specs=[far, far, far, far,...]
where the time goes in v4:
time: 85 us; the launch traced here: 84.7 us
  Pallas kernels  84.1 us (99%)
    pallas_call x1, Pallas kernels, shards(): pl.pallas_call(kernel, out_shape=out_shape, in_specs=[far, far, far, far,...  82.3 us
    pallas_call x1, Pallas kernels, shards(): pl.pallas_call(copy_kernel, out_shape=out_shape, in_specs=[near, near], o...  1.84 us

profile of v4, /device:TPU:1, one launch (start us, length us, event | category | flops | bytes accessed | tf_op | source)
XLA Modules:
  0.0 84.7 jit_solution(2665047021357704809)
XLA Ops:
  0.6 82.3 %shard_map.86 = (bf16[128,1024]{1,0:T(8,128)(2,1)}, bf16[128,1024]{1,0:T(8,128)(2,1)}) custom-call(bf16[128,1024]{1,0:T(8,128)(2,1)} %refs_0_.1, bf16[128,1024]{1,0:T(8,128)(2,1)} %refs_1_.1, bf16[1024,3072]{1,0:T(8,128)(2,1)} %refs_2_.1, bf16[1024,1024]{1,0:T(8,128)(2,1)} %refs_3_.1, s32[8,8]{1,0:T(8,128)} %refs_4_.1, s32[8]{0:T(128)} %refs_5_.1, ...), custom_call_target="tpu_custom_call" | custom-call | tf_op jit(solution)/shard_map/pallas_call | solution.py:525
  82.9 1.8 %shard_map.87 = (bf16[128,1024]{1,0:T(8,128)(2,1)}, bf16[128,1024]{1,0:T(8,128)(2,1)}) custom-call(bf16[128,1024]{1,0:T(8,128)(2,1)} %get-tuple-element.4.attended, bf16[128,1024]{1,0:T(8,128)(2,1)} %get-tuple-element.5.grad_features), custom_call_target="tpu_custom_call" | custom-call | tf_op jit(solution)/shard_map/pallas_call | solution.py:538

commit v5 on v4

--- a/solution.py
+++ b/solution.py
@@ -146,39 +146,45 @@
         copy.start()
         return copy
 
+    def spread_copy(hh, part, src, e, blocks, to):
+        if hh == 0:
+            source = refs["spread"][part][src - 1] if src else refs["y_out"][part][0]
+            target = refs["spread"][part][e - 1]
+        else:
+            source, target = first[part][1][src], first[part][1][e]
+        return remote(
+            source.at[blocks], target.at[blocks],
+            refs["f_send"].at[hh, part], refs["f_recv"].at[hh, part, e - 1],
+            (at(part, to, 0), h),
+        )
+
+    def spread_start(hh, part):
+        for e in (1, 3):
+            spread_copy(hh, part, 0, e, pl.ds(0, NB), back_by(e)).start()
+
+    def spread_done(hh, part, e):
+        spread_copy(hh, part, 0, e, pl.ds(0, NB), e).wait_recv()
+        if e == 1:
+            spread_copy(hh, part, 1, 2, pl.ds(0, NB // 2), 3).start()
+        if e == 3:
+            spread_copy(hh, part, 3, 2, pl.ds(NB // 2, NB // 2), 1).start()
+
     index_copy = index_tables()
     load_feat.wait()
     load_k.wait()
     project(feat, refs["w"][0], NN, put_heads(0))
     pl.semaphore_wait(barrier, 6 + NB - 1)
+    spread_start(0, 0)
     y_start(0, refs["y_out"][0][0], first[0][0][0])
     load_gout.start()
     load_q.start()
     load_o.start()
     load_v.wait()
     project(feat, refs["w"][1], NN, put_heads(1))
+    spread_start(0, 1)
     y_start(2, refs["y_out"][1][0], first[1][0][0])
     y_start(1, refs["y_out"][0][1], first[0][1][0])
     y_start(3, refs["y_out"][1][1], first[1][1][0])
-    load_q.wait()
-    project(feat, refs["w"][2], NN, put_whole(0))
-    y_start(4, refs["qg_out"][0], refs["qg"][0])
-    load_gout.wait()
-    load_o.wait()
-    project(gout, refs["w"][3], NT, put_whole(1))
-    y_start(5, refs["qg_out"][1], refs["qg"][1])
-    index_copy.wait()
-
-    def spread_copy(hh, part, src, e, blocks, to):
-        return remote(
-            first[part][hh][src].at[blocks], first[part][hh][e].at[blocks],
-            refs["f_send"].at[hh, part], refs["f_recv"].at[hh, part, e - 1],
-            (at(part, to, 0), h),
-        )
-
-    def spread_wait(hh, part, e):
-        spread_copy(hh, part, 0, e, pl.ds(0, NB), e).wait_recv()
-
     def pick_copy(hh, part, d, e):
         return remote(
             stage[part][hh].at[d - 1, e],
@@ -204,24 +210,36 @@
             for r in range(SLOT):
                 table[part][hh][base(part, 0, e) + r] = first[part][hh][e][fetch[r, c, source]]
 
-    def forward_start(hh):
-        for part in range(2):
-            y_wait(2 * part + hh, refs["y_out"][part][hh], first[part][hh][0])
-            for e in (1, 3):
-                spread_copy(hh, part, 0, e, pl.ds(0, NB), back_by(e)).start()
-            pick(hh, part, 0)
-        for part in range(2):
-            keep(hh, part, 0)
-
-    def forward_step(hh, e):
-        for part in range(2):
-            spread_wait(hh, part, e)
-            if e == 1:
-                spread_copy(hh, part, 1, 2, pl.ds(0, NB // 2), 3).start()
-            if e == 3:
-                spread_copy(hh, part, 3, 2, pl.ds(NB // 2, NB // 2), 1).start()
-            pick(hh, part, e)
-            keep(hh, part, e)
+    def far_kind(part, e):
+        return 12 + 3 * part + e - 1
+
+    def forward_first(e):
+        for part in range(2):
+            spread_done(0, part, e)
+            y_start(far_kind(part, e), refs["spread"][part][e - 1], first[part][0][e])
+
+    def forward_second(e):
+        for part in range(2):
+            kind = far_kind(part, e) if e else 2 * part
+            source = refs["spread"][part][e - 1] if e else refs["y_out"][part][0]
+            y_wait(kind, source, first[part][0][e])
+            pick(0, part, e)
+        for part in range(2):
+            keep(0, part, e)
+
+    def forward_start():
+        for part in range(2):
+            y_wait(2 * part + 1, refs["y_out"][part][1], first[part][1][0])
+            spread_start(1, part)
+        for part in range(2):
+            pick(1, part, 0)
+            keep(1, part, 0)
+
+    def forward_step(e):
+        for part in range(2):
+            spread_done(1, part, e)
+            pick(1, part, e)
+            keep(1, part, e)
 
     def stand_in(part, hh, send, recv, blocks):
         some = table[part][hh].at[pl.ds(0, blocks)]
@@ -329,12 +347,26 @@
 
             lax.fori_loop(0, NB, own, 0)
 
+    def back_kind(part, e):
+        return 18 + 3 * part + e - 1 if e else 9 + 2 * part
+
+    def exchanged(part, e):
+        return refs["turned"][part][e - 1] if e else refs["grads"][part][1]
+
     def back_copy(hh, part, e):
         return remote(
-            back_out[part][hh].at[e - 1], back_in[part][hh].at[e - 1],
+            back_out[part][0].at[e - 1] if hh == 0 else exchanged(part, e),
+            back_in[part][hh].at[e - 1],
             refs["b_send"].at[hh, part], refs["b_recv"].at[hh, part],
             (at(part, e, 0), h),
         )
+
+    def backward_turn(e):
+        for part in range(2):
+            out = final[part][1] if e == 0 else back_out[part][1].at[e - 1]
+            y_wait(back_kind(part, e), out, exchanged(part, e))
+            if e:
+                back_copy(1, part, e).start()
 
     def backward_step(hh, e):
         for part in range(2):
@@ -345,7 +377,9 @@
             ).wait_recv()
             source = at(part, e, 0)
 
-            def one(t, _, part=part, source=source):
+            out = final[part][1] if e == 0 else back_out[part][hh].at[e - 1]
+
+            def one(t, _, part=part, source=source, out=out):
                 acc = own_sum[part][hh][t] if e == 0 else None
                 for d in (0, 1, 2, 3):
                     if d == 0 and e == 0:
@@ -357,46 +391,60 @@
                         place = jnp.where(fetch[r, reader, source] == t, here, place)
                     term = got[part][hh][e][place].astype(F32)
                     acc = term if acc is None else acc + term
-                if e == 0:
+                if e == 0 and hh == 0:
                     own_sum[part][hh][t] = acc
                 else:
-                    back_out[part][hh][e - 1, t] = acc.astype(BF)
+                    out[t] = acc.astype(BF)
                 return 0
 
             lax.fori_loop(0, NB, one, 0)
-            if e:
+            if hh == 1:
+                y_start(back_kind(part, e), out, exchanged(part, e))
+            elif e:
                 back_copy(hh, part, e).start()
 
-    def backward_finish(hh):
-        for part in range(2):
-            stand_in(part, hh, refs["b_send"], refs["b_recv"], 3 * NB).wait_recv()
+    def backward_finish():
+        for part in range(2):
+            stand_in(part, 0, refs["b_send"], refs["b_recv"], 3 * NB).wait_recv()
 
             def one(t, _, part=part):
-                acc = own_sum[part][hh][t]
+                acc = own_sum[part][0][t]
                 for e in range(3):
-                    acc = acc + back_in[part][hh][e, t].astype(F32)
-                final[part][hh][t] = acc.astype(BF)
+                    acc = acc + back_in[part][0][e, t].astype(F32)
+                final[part][0][t] = acc.astype(BF)
                 return 0
 
             lax.fori_loop(0, NB, one, 0)
-            y_start(8 + 2 * part + hh, final[part][hh], refs["grads"][part][hh])
-
-    forward_start(0)
-    for e in NEAR:
-        forward_step(0, e)
-    forward_start(1)
+            y_start(8 + 2 * part, final[part][0], refs["grads"][part][0])
+
+    load_q.wait()
+    project(feat, refs["w"][2], NN, put_whole(0))
+    forward_second(0)
+    forward_first(1)
+    forward_first(3)
+    forward_start()
+    forward_first(2)
+    load_gout.wait()
+    load_o.wait()
+    project(gout, refs["w"][3], NT, put_whole(1))
+    y_start(4, refs["qg_out"][0], refs["qg"][0])
+    y_start(5, refs["qg_out"][1], refs["qg"][1])
+    index_copy.wait()
+    forward_second(1)
+    forward_second(3)
+    forward_second(2)
     for part in range(2):
         terms[part][LIVE] = jnp.zeros((HD, BLK), F32)
         for hh in range(2):
             for e in range(SIDE):
                 got[part][hh][e][12] = jnp.zeros((HD, BLK), BF)
+    forward_step(1)
+    forward_step(3)
     y_wait(4, refs["qg_out"][0], refs["qg"][0])
     y_wait(5, refs["qg_out"][1], refs["qg"][1])
-    forward_step(1, 1)
-    forward_step(1, 3)
     forward_done(0)
     attention(0)
-    forward_step(1, 2)
+    forward_step(2)
     backward_start(0)
     forward_done(1)
     attention(1)
@@ -405,7 +453,6 @@
     y_start(7, refs["row_out"][1], refs["rows"][1])
     for e in OUTWARD:
         backward_step(0, e)
-    backward_finish(0)
 
     def wide(ref):
         return jnp.concatenate([ref[i] for i in range(NB)], axis=1)
@@ -413,8 +460,11 @@
     def wide_t(part):
         tiles = []
         for i in range(NB):
-            tile = jnp.concatenate([refs["grads"][part][hh][i] for hh in range(2)], axis=0)
-            tiles.append(tile.astype(F32).T.astype(BF))
+            late = refs["grads"][part][1][i].astype(F32)
+            for e in range(3):
+                late = late + back_in[part][1][e, i].astype(F32)
+            tile = jnp.concatenate([refs["grads"][part][0][i].astype(F32), late], axis=0)
+            tiles.append(tile.T.astype(BF))
         return jnp.concatenate(tiles, axis=1)
 
     y_wait(6, refs["row_out"][0], refs["rows"][0])
@@ -425,10 +475,12 @@
     refs["grad"][...] = dot(wide(refs["rows"][1]), refs["w"][2][...], NT)
     for e in OUTWARD:
         backward_step(1, e)
-    backward_finish(1)
+    backward_finish()
+    for e in OUTWARD:
+        backward_turn(e)
     for part in range(2):
-        for hh in range(2):
-            y_wait(8 + 2 * part + hh, final[part][hh], refs["grads"][part][hh])
+        y_wait(8 + 2 * part, final[part][0], refs["grads"][part][0])
+        stand_in(part, 1, refs["b_send"], refs["b_recv"], 3 * NB).wait_recv()
         term = dot(wide_t(part), refs["w"][part][...], NT)
         if part == 0:
             refs["grad"][...] += term
@@ -442,6 +494,15 @@
         for hh in range(2):
             y_all(2 * part + hh, refs["y_out"][part][hh], first[part][hh][0]).wait_send()
             y_all(8 + 2 * part + hh, final[part][hh], refs["grads"][part][hh]).wait_send()
+            for e in (1, 2, 3):
+                if hh == 0:
+                    y_all(
+                        far_kind(part, e), refs["spread"][part][e - 1], first[part][0][e]
+                    ).wait_send()
+                else:
+                    y_all(
+                        back_kind(part, e), back_out[part][1].at[e - 1], exchanged(part, e)
+                    ).wait_send()
             for name, blocks in (("f", 24), ("s", 36), ("g", 36), ("b", 24)):
                 stand_in(part, hh, refs[name + "_send"], refs["s_recv"], blocks).wait_send()
     save_att.wait()
@@ -479,6 +540,8 @@
         "qg_out": each(lambda: vm(NB, BLK, BLK), 2),
         "qg": each(lambda: vm(NB, BLK, BLK), 2),
         "first": each(lambda: vm(NB, *tile), 2, 2, SIDE),
+        "spread": each(lambda: vm(NB, *tile), 2, 3),
+        "turned": each(lambda: vm(NB, *tile), 2, 3),
         "table": each(lambda: vm(TABLE, *tile), 2, 2),
         "stage": each(lambda: vm(3, SIDE, SLOT, *tile), 2, 2),
         "terms": each(lambda: vm(LIVE + 1, *tile, dtype=F32), 2),
@@ -500,8 +563,8 @@
         "index_v": vm(2 * NB, BLK, dtype=jnp.int32),
         "index": pltpu.SMEM((2 * NB, BLK), jnp.int32),
         "w_sem": dma((7,)),
-        "y_send": dma((12,)),
-        "y_recv": dma((12,)),
+        "y_send": dma((24,)),
+        "y_recv": dma((24,)),
         "f_send": dma((2, 2)),
         "f_recv": dma((2, 2, 3)),
         "s_send": dma((2, 2)),

time: 85 us -> 78.5 us (0.924)
  Pallas kernels: 84.1 us -> 77.6 us
    pallas_call x1, Pallas kernels: 82.3 us -> 75.8 us  [shards(): pl.pallas_call(kernel, out_shape=out_shape, in_specs=[far, far, far, far,...]
where the time goes in v5:
time: 78.5 us; the launch traced here: 78.3 us
  Pallas kernels  77.6 us (99%)
    pallas_call x1, Pallas kernels, shards(): pl.pallas_call(kernel, out_shape=out_shape, in_specs=[far, far, far, far,...  75.8 us
    pallas_call x1, Pallas kernels, shards(): pl.pallas_call(copy_kernel, out_shape=out_shape, in_specs=[near, near], o...  1.84 us

profile of v5, /device:TPU:1, one launch (start us, length us, event | category | flops | bytes accessed | tf_op | source)
XLA Modules:
  0.0 78.3 jit_solution(6475607347403145500)
XLA Ops:
  0.6 75.8 %shard_map.86 = (bf16[128,1024]{1,0:T(8,128)(2,1)}, bf16[128,1024]{1,0:T(8,128)(2,1)}) custom-call(bf16[128,1024]{1,0:T(8,128)(2,1)} %refs_0_.1, bf16[128,1024]{1,0:T(8,128)(2,1)} %refs_1_.1, bf16[1024,3072]{1,0:T(8,128)(2,1)} %refs_2_.1, bf16[1024,1024]{1,0:T(8,128)(2,1)} %refs_3_.1, s32[8,8]{1,0:T(8,128)} %refs_4_.1, s32[8]{0:T(128)} %refs_5_.1, ...), custom_call_target="tpu_custom_call" | custom-call | tf_op jit(solution)/shard_map/pallas_call | solution.py:588
  76.4 1.8 %shard_map.87 = (bf16[128,1024]{1,0:T(8,128)(2,1)}, bf16[128,1024]{1,0:T(8,128)(2,1)}) custom-call(bf16[128,1024]{1,0:T(8,128)(2,1)} %get-tuple-element.4.attended, bf16[128,1024]{1,0:T(8,128)(2,1)} %get-tuple-element.5.grad_features), custom_call_target="tpu_custom_call" | custom-call | tf_op jit(solution)/shard_map/pallas_call | solution.py:601

commit v6 on v5

--- a/solution.py
+++ b/solution.py
@@ -106,18 +106,34 @@
             put(2 * p, out[:, :BLK].T.astype(BF))
             put(2 * p + 1, out[:, BLK:].T.astype(BF))
 
-    def put_heads(part):
+    def put_heads(outs):
         def put(dest, tile):
-            refs["y_out"][part][0][dest] = tile[:HD]
-            refs["y_out"][part][1][dest] = tile[HD:]
+            outs[0][dest] = tile[:HD]
+            outs[1][dest] = tile[HD:]
 
         return put
 
-    def put_whole(n):
-        def put(dest, tile):
-            refs["qg_out"][n][dest] = tile
-
-        return put
+    def qg_kind(n, hh):
+        return 24 + n if hh else 4 + n
+
+    def qg_start(hh):
+        for n in range(2):
+            y_start(qg_kind(n, hh), refs["qg_out"][n][hh], refs["qg"][n][hh])
+
+    def row_kind(n, hh):
+        return 26 + n if hh else 6 + n
+
+    def rows_start(hh):
+        for n in range(2):
+            y_start(row_kind(n, hh), refs["row_out"][n][hh], refs["rows"][n][hh])
+
+    def rows_wait(n):
+        for hh in range(2):
+            y_wait(row_kind(n, hh), refs["row_out"][n][hh], refs["rows"][n][hh])
+
+    def qg_wait(hh):
+        for n in range(2):
+            y_wait(qg_kind(n, hh), refs["qg_out"][n][hh], refs["qg"][n][hh])
 
     def index_tables():
         kept = refs["kept"][...]
@@ -164,6 +180,9 @@
 
     def spread_done(hh, part, e):
         spread_copy(hh, part, 0, e, pl.ds(0, NB), e).wait_recv()
+        spread_relay(hh, part, e)
+
+    def spread_relay(hh, part, e):
         if e == 1:
             spread_copy(hh, part, 1, 2, pl.ds(0, NB // 2), 3).start()
         if e == 3:
@@ -172,7 +191,7 @@
     index_copy = index_tables()
     load_feat.wait()
     load_k.wait()
-    project(feat, refs["w"][0], NN, put_heads(0))
+    project(feat, refs["w"][0], NN, put_heads(refs["y_out"][0]))
     pl.semaphore_wait(barrier, 6 + NB - 1)
     spread_start(0, 0)
     y_start(0, refs["y_out"][0][0], first[0][0][0])
@@ -180,7 +199,7 @@
     load_q.start()
     load_o.start()
     load_v.wait()
-    project(feat, refs["w"][1], NN, put_heads(1))
+    project(feat, refs["w"][1], NN, put_heads(refs["y_out"][1]))
     spread_start(0, 1)
     y_start(2, refs["y_out"][1][0], first[1][0][0])
     y_start(1, refs["y_out"][0][1], first[0][1][0])
@@ -235,9 +254,14 @@
             pick(1, part, 0)
             keep(1, part, 0)
 
+    def forward_relay(e):
+        for part in range(2):
+            spread_done(1, part, e)
+
     def forward_step(e):
         for part in range(2):
-            spread_done(1, part, e)
+            if e == 2:
+                spread_done(1, part, e)
             pick(1, part, e)
             keep(1, part, e)
 
@@ -250,14 +274,12 @@
             stand_in(part, hh, refs["s_send"], refs["s_recv"], 3 * SIDE * SLOT).wait_recv()
 
     def attention(hh):
-        half = slice(hh * HD, (hh + 1) * HD)
-
         def load_block(b):
             slots = [index[b, j] for j in range(NB)]
             kc = jnp.concatenate([table[0][hh][i] for i in slots], axis=1)
             vc = jnp.concatenate([table[1][hh][i] for i in slots], axis=1)
-            q_t = refs["qg"][0][b, half, :].astype(F32) * 0.125
-            g_t = refs["qg"][1][b, half, :].astype(F32)
+            q_t = refs["qg"][0][hh][b].astype(F32) * 0.125
+            g_t = refs["qg"][1][hh][b].astype(F32)
             return kc, vc, q_t, g_t
 
         def block(i, _):
@@ -288,19 +310,15 @@
                 delta = jnp.sum(g * attn.astype(F32), axis=1, keepdims=True)
                 grads.append((a * (dot(g.astype(BF), vc) - delta)).astype(BF))
             for b, low, ds, attn, (kc, vc, q_t, g_t) in zip(blocks, lows, grads, attns, loaded):
-                dq = (dot(ds, kc, NT) * 0.125).astype(BF)
+                dq = dot(ds, kc, NT) * 0.125
                 dk_t = dot(q_t.astype(BF), ds)
                 dv_t = dot(g_t.astype(BF), low)
                 for j in range(NB):
                     cols = slice(j * BLK, (j + 1) * BLK)
                     terms[0][b * NB + j] = dk_t[:, cols]
                     terms[1][b * NB + j] = dv_t[:, cols]
-                if hh == 0:
-                    refs["half"][0][b] = attn
-                    refs["half"][1][b] = dq
-                else:
-                    refs["row_out"][0][b] = jnp.concatenate([refs["half"][0][b], attn], axis=1)
-                    refs["row_out"][1][b] = jnp.concatenate([refs["half"][1][b], dq], axis=1)
+                refs["row_out"][0][hh][b] = attn.astype(F32).T.astype(BF)
+                refs["row_out"][1][hh][b] = dq.T.astype(BF)
             return 0
 
         lax.fori_loop(0, NB // GROUP, block, 0)
@@ -418,7 +436,7 @@
             y_start(8 + 2 * part, final[part][0], refs["grads"][part][0])
 
     load_q.wait()
-    project(feat, refs["w"][2], NN, put_whole(0))
+    project(feat, refs["w"][2], NN, put_heads(refs["qg_out"][0]))
     forward_second(0)
     forward_first(1)
     forward_first(3)
@@ -426,36 +444,41 @@
     forward_first(2)
     load_gout.wait()
     load_o.wait()
-    project(gout, refs["w"][3], NT, put_whole(1))
-    y_start(4, refs["qg_out"][0], refs["qg"][0])
-    y_start(5, refs["qg_out"][1], refs["qg"][1])
+    project(gout, refs["w"][3], NT, put_heads(refs["qg_out"][1]))
+    qg_start(0)
+    qg_start(1)
     index_copy.wait()
     forward_second(1)
     forward_second(3)
+    forward_relay(1)
+    forward_relay(3)
     forward_second(2)
     for part in range(2):
         terms[part][LIVE] = jnp.zeros((HD, BLK), F32)
         for hh in range(2):
             for e in range(SIDE):
                 got[part][hh][e][12] = jnp.zeros((HD, BLK), BF)
-    forward_step(1)
-    forward_step(3)
-    y_wait(4, refs["qg_out"][0], refs["qg"][0])
-    y_wait(5, refs["qg_out"][1], refs["qg"][1])
+    for e in NEAR:
+        forward_step(e)
+    qg_wait(0)
     forward_done(0)
     attention(0)
-    forward_step(2)
+    rows_start(0)
     backward_start(0)
     forward_done(1)
+    qg_wait(1)
     attention(1)
     backward_start(1)
-    y_start(6, refs["row_out"][0], refs["rows"][0])
-    y_start(7, refs["row_out"][1], refs["rows"][1])
+    rows_start(1)
     for e in OUTWARD:
         backward_step(0, e)
 
-    def wide(ref):
-        return jnp.concatenate([ref[i] for i in range(NB)], axis=1)
+    def wide_rows(n):
+        tiles = []
+        for i in range(NB):
+            tile = jnp.concatenate([refs["rows"][n][hh][i] for hh in range(2)], axis=0)
+            tiles.append(tile.astype(F32).T.astype(BF))
+        return jnp.concatenate(tiles, axis=1)
 
     def wide_t(part):
         tiles = []
@@ -467,17 +490,21 @@
             tiles.append(tile.T.astype(BF))
         return jnp.concatenate(tiles, axis=1)
 
-    y_wait(6, refs["row_out"][0], refs["rows"][0])
-    refs["att"][...] = dot(wide(refs["rows"][0]), refs["w"][3][...]).astype(BF)
+    backward_step(1, 2)
+    rows_wait(0)
+    refs["att"][...] = dot(wide_rows(0), refs["w"][3][...]).astype(BF)
     save_att = load(0, refs["att"], refs["attended"])
     save_att.start()
-    y_wait(7, refs["row_out"][1], refs["rows"][1])
-    refs["grad"][...] = dot(wide(refs["rows"][1]), refs["w"][2][...], NT)
-    for e in OUTWARD:
-        backward_step(1, e)
+    backward_step(1, 1)
+    rows_wait(1)
+    refs["grad"][...] = dot(wide_rows(1), refs["w"][2][...], NT)
+    backward_step(1, 3)
+    backward_turn(2)
+    backward_step(1, 0)
+    backward_turn(1)
+    backward_turn(3)
     backward_finish()
-    for e in OUTWARD:
-        backward_turn(e)
+    backward_turn(0)
     for part in range(2):
         y_wait(8 + 2 * part, final[part][0], refs["grads"][part][0])
         stand_in(part, 1, refs["b_send"], refs["b_recv"], 3 * NB).wait_recv()
@@ -489,8 +516,9 @@
     save_gf = load(1, refs["gf"], refs["grad_features"])
     save_gf.start()
     for part in range(2):
-        y_all(4 + part, refs["qg_out"][part], refs["qg"][part]).wait_send()
-        y_all(6 + part, refs["row_out"][part], refs["rows"][part]).wait_send()
+        for hh in range(2):
+            y_all(qg_kind(part, hh), refs["qg_out"][part][hh], refs["qg"][part][hh]).wait_send()
+            y_all(row_kind(part, hh), refs["row_out"][part][hh], refs["rows"][part][hh]).wait_send()
         for hh in range(2):
             y_all(2 * part + hh, refs["y_out"][part][hh], first[part][hh][0]).wait_send()
             y_all(8 + 2 * part + hh, final[part][hh], refs["grads"][part][hh]).wait_send()
@@ -537,17 +565,16 @@
     layout = {
         "w": each(lambda: vm(1024, 1024), 4),
         "y_out": each(lambda: vm(NB, *tile), 2, 2),
-        "qg_out": each(lambda: vm(NB, BLK, BLK), 2),
-        "qg": each(lambda: vm(NB, BLK, BLK), 2),
+        "qg_out": each(lambda: vm(NB, *tile), 2, 2),
+        "qg": each(lambda: vm(NB, *tile), 2, 2),
         "first": each(lambda: vm(NB, *tile), 2, 2, SIDE),
         "spread": each(lambda: vm(NB, *tile), 2, 3),
         "turned": each(lambda: vm(NB, *tile), 2, 3),
         "table": each(lambda: vm(TABLE, *tile), 2, 2),
         "stage": each(lambda: vm(3, SIDE, SLOT, *tile), 2, 2),
         "terms": each(lambda: vm(LIVE + 1, *tile, dtype=F32), 2),
-        "half": each(lambda: vm(NB, BLK, HD), 2),
-        "row_out": each(lambda: vm(NB, BLK, BLK), 2),
-        "rows": each(lambda: vm(NB, BLK, BLK), 2),
+        "row_out": each(lambda: vm(NB, *tile), 2, 2),
+        "rows": each(lambda: vm(NB, *tile), 2, 2),
         "slot_out": each(lambda: vm(3, SIDE, SLOT, *tile), 2, 2),
         "got": each(lambda: vm(13, *tile), 2, 2, SIDE),
         "own_sum": each(lambda: vm(NB, *tile, dtype=F32), 2, 2),
@@ -563,8 +590,8 @@
         "index_v": vm(2 * NB, BLK, dtype=jnp.int32),
         "index": pltpu.SMEM((2 * NB, BLK), jnp.int32),
         "w_sem": dma((7,)),
-        "y_send": dma((24,)),
-        "y_recv": dma((24,)),
+        "y_send": dma((28,)),
+        "y_recv": dma((28,)),
         "f_send": dma((2, 2)),
         "f_recv": dma((2, 2, 3)),
         "s_send": dma((2, 2)),

time: 78.5 us -> 75.3 us (0.959)
  Pallas kernels: 77.6 us -> 74.5 us
    pallas_call x1, Pallas kernels: 75.8 us -> 72.6 us  [shards(): pl.pallas_call(kernel, out_shape=out_shape, in_specs=[far, far, far, far,...]
where the time goes in v6:
time: 75.3 us; the launch traced here: 75.1 us
  Pallas kernels  74.5 us (99%)
    pallas_call x1, Pallas kernels, shards(): pl.pallas_call(kernel, out_shape=out_shape, in_specs=[far, far, far, far,...  72.6 us
    pallas_call x1, Pallas kernels, shards(): pl.pallas_call(copy_kernel, out_shape=out_shape, in_specs=[near, near], o...  1.84 us

profile of v6, /device:TPU:1, one launch (start us, length us, event | category | flops | bytes accessed | tf_op | source)
XLA Modules:
  0.0 75.1 jit_solution(6113465987774294551)
XLA Ops:
  0.6 72.6 %shard_map.86 = (bf16[128,1024]{1,0:T(8,128)(2,1)}, bf16[128,1024]{1,0:T(8,128)(2,1)}) custom-call(bf16[128,1024]{1,0:T(8,128)(2,1)} %refs_0_.1, bf16[128,1024]{1,0:T(8,128)(2,1)} %refs_1_.1, bf16[1024,3072]{1,0:T(8,128)(2,1)} %refs_2_.1, bf16[1024,1024]{1,0:T(8,128)(2,1)} %refs_3_.1, s32[8,8]{1,0:T(8,128)} %refs_4_.1, s32[8]{0:T(128)} %refs_5_.1, ...), custom_call_target="tpu_custom_call" | custom-call | tf_op jit(solution)/shard_map/pallas_call | solution.py:615
  73.3 1.8 %shard_map.87 = (bf16[128,1024]{1,0:T(8,128)(2,1)}, bf16[128,1024]{1,0:T(8,128)(2,1)}) custom-call(bf16[128,1024]{1,0:T(8,128)(2,1)} %get-tuple-element.4.attended, bf16[128,1024]{1,0:T(8,128)(2,1)} %get-tuple-element.5.grad_features), custom_call_target="tpu_custom_call" | custom-call | tf_op jit(solution)/shard_map/pallas_call | solution.py:628

commit v7 on v6

--- a/solution.py
+++ b/solution.py
@@ -175,7 +175,7 @@
         )
 
     def spread_start(hh, part):
-        for e in (1, 3):
+        for e in NEAR if hh == 0 else (1, 3):
             spread_copy(hh, part, 0, e, pl.ds(0, NB), back_by(e)).start()
 
     def spread_done(hh, part, e):
@@ -183,6 +183,8 @@
         spread_relay(hh, part, e)
 
     def spread_relay(hh, part, e):
+        if hh == 0:
+            return
         if e == 1:
             spread_copy(hh, part, 1, 2, pl.ds(0, NB // 2), 3).start()
         if e == 3:

time: 75.3 us -> 73.4 us (0.975)
  Pallas kernels: 74.5 us -> 72.6 us
    pallas_call x1, Pallas kernels: 72.6 us -> 70.7 us  [shards(): pl.pallas_call(kernel, out_shape=out_shape, in_specs=[far, far, far, far,...]
where the time goes in v7:
time: 73.4 us; the launch traced here: 73.2 us
  Pallas kernels  72.6 us (99%)
    pallas_call x1, Pallas kernels, shards(): pl.pallas_call(kernel, out_shape=out_shape, in_specs=[far, far, far, far,...  70.7 us
    pallas_call x1, Pallas kernels, shards(): pl.pallas_call(copy_kernel, out_shape=out_shape, in_specs=[near, near], o...  1.84 us

profile of v7, /device:TPU:1, one launch (start us, length us, event | category | flops | bytes accessed | tf_op | source)
XLA Modules:
  0.0 73.2 jit_solution(12060288986637569660)
XLA Ops:
  0.6 70.7 %shard_map.86 = (bf16[128,1024]{1,0:T(8,128)(2,1)}, bf16[128,1024]{1,0:T(8,128)(2,1)}) custom-call(bf16[128,1024]{1,0:T(8,128)(2,1)} %refs_0_.1, bf16[128,1024]{1,0:T(8,128)(2,1)} %refs_1_.1, bf16[1024,3072]{1,0:T(8,128)(2,1)} %refs_2_.1, bf16[1024,1024]{1,0:T(8,128)(2,1)} %refs_3_.1, s32[8,8]{1,0:T(8,128)} %refs_4_.1, s32[8]{0:T(128)} %refs_5_.1, ...), custom_call_target="tpu_custom_call" | custom-call | tf_op jit(solution)/shard_map/pallas_call | solution.py:617
  71.4 1.8 %shard_map.87 = (bf16[128,1024]{1,0:T(8,128)(2,1)}, bf16[128,1024]{1,0:T(8,128)(2,1)}) custom-call(bf16[128,1024]{1,0:T(8,128)(2,1)} %get-tuple-element.4.attended, bf16[128,1024]{1,0:T(8,128)(2,1)} %get-tuple-element.5.grad_features), custom_call_target="tpu_custom_call" | custom-call | tf_op jit(solution)/shard_map/pallas_call | solution.py:630

commit v8 on v7

--- a/solution.py
+++ b/solution.py
@@ -62,7 +62,6 @@
     load_feat, load_gout, load_k, load_v, load_q, load_o = loads
     load_feat.start()
     load_k.start()
-    load_v.start()
 
     barrier = pltpu.get_barrier_semaphore()
     for d in (1, 2, 3):
@@ -190,9 +189,9 @@
         if e == 3:
             spread_copy(hh, part, 3, 2, pl.ds(NB // 2, NB // 2), 1).start()
 
-    index_copy = index_tables()
     load_feat.wait()
     load_k.wait()
+    load_v.start()
     project(feat, refs["w"][0], NN, put_heads(refs["y_out"][0]))
     pl.semaphore_wait(barrier, 6 + NB - 1)
     spread_start(0, 0)
@@ -206,6 +205,7 @@
     y_start(2, refs["y_out"][1][0], first[1][0][0])
     y_start(1, refs["y_out"][0][1], first[0][1][0])
     y_start(3, refs["y_out"][1][1], first[1][1][0])
+    index_copy = index_tables()
     def pick_copy(hh, part, d, e):
         return remote(
             stage[part][hh].at[d - 1, e],
@@ -451,9 +451,9 @@
     qg_start(1)
     index_copy.wait()
     forward_second(1)
-    forward_second(3)
     forward_relay(1)
     forward_relay(3)
+    forward_second(3)
     forward_second(2)
     for part in range(2):
         terms[part][LIVE] = jnp.zeros((HD, BLK), F32)

time: 73.4 us -> 74.6 us (1.016)
  Pallas kernels: 72.6 us -> 73.7 us
    pallas_call x1, Pallas kernels: 70.7 us -> 71.9 us  [shards(): pl.pallas_call(kernel, out_shape=out_shape, in_specs=[far, far, far, far,...]
where the time goes in v8:
time: 74.6 us; the launch traced here: 74.4 us
  Pallas kernels  73.7 us (99%)
    pallas_call x1, Pallas kernels, shards(): pl.pallas_call(kernel, out_shape=out_shape, in_specs=[far, far, far, far,...  71.9 us
    pallas_call x1, Pallas kernels, shards(): pl.pallas_call(copy_kernel, out_shape=out_shape, in_specs=[near, near], o...  1.84 us

profile of v8, /device:TPU:1, one launch (start us, length us, event | category | flops | bytes accessed | tf_op | source)
XLA Modules:
  0.0 74.4 jit_solution(15682161752728001354)
XLA Ops:
  0.6 71.9 %shard_map.86 = (bf16[128,1024]{1,0:T(8,128)(2,1)}, bf16[128,1024]{1,0:T(8,128)(2,1)}) custom-call(bf16[128,1024]{1,0:T(8,128)(2,1)} %refs_0_.1, bf16[128,1024]{1,0:T(8,128)(2,1)} %refs_1_.1, bf16[1024,3072]{1,0:T(8,128)(2,1)} %refs_2_.1, bf16[1024,1024]{1,0:T(8,128)(2,1)} %refs_3_.1, s32[8,8]{1,0:T(8,128)} %refs_4_.1, s32[8]{0:T(128)} %refs_5_.1, ...), custom_call_target="tpu_custom_call" | custom-call | tf_op jit(solution)/shard_map/pallas_call | solution.py:617
  72.5 1.8 %shard_map.87 = (bf16[128,1024]{1,0:T(8,128)(2,1)}, bf16[128,1024]{1,0:T(8,128)(2,1)}) custom-call(bf16[128,1024]{1,0:T(8,128)(2,1)} %get-tuple-element.4.attended, bf16[128,1024]{1,0:T(8,128)(2,1)} %get-tuple-element.5.grad_features), custom_call_target="tpu_custom_call" | custom-call | tf_op jit(solution)/shard_map/pallas_call | solution.py:630
